TPU v7x, 128 devices: a whole 4x4x4 slice. The times are simulated.
128 devices in a mesh: dp: 8 (over y, core), mp: 16 (over z, x).
Axes of the slice: x: 4, y: 4, z: 4, core: 2. Of those that a mesh axis runs over, the one named last changes fastest.
Arguments:
- local_grads: bfloat16 [8, 64, 1024, 1024], P('dp', 'mp'), may hold values from -8 to 8
- left_root: bfloat16 [16, 8, 1024, 1024], P('mp', 'dp'), may hold values from -1 to 3
- right_root: bfloat16 [16, 8, 1024, 1024], P('mp', 'dp'), may hold values from -1 to 3
- accumulator: float32 [64, 1024, 1024], P('mp', 'dp'), may hold values from 0.5 to 5
- momentum: bfloat16 [64, 1024, 1024], P('mp', 'dp'), may hold values from -3 to 3
- block_owner: int32 [64], replicated, may hold values from 0 to 15, as said below
- block_slot: int32 [64], replicated, may hold values from 0 to 7, as said below
Outputs:
- new_accumulator: float32 [64, 1024, 1024], P('mp', 'dp')
- update: bfloat16 [64, 1024, 1024], P('mp')
Inputs may be any that keep to these rules, and one draw needn't show every extreme that they name: `block_owner`: block m * 4 + j is block j of tensor-parallel shard m. The blocks of one shard have different owners. No owner holds more than 8 blocks, and some owner holds exactly 8. `block_slot`: two blocks with the same owner have different slots.
All inputs are finite; a program needn't handle non-finite values.
Results may differ from a plain program's by a relative error of at most 0.027.
Values may be sent and summed in bfloat16 or wider, within the bound.
A program may use at most 128 MiB of HBM per device.

v0:
```python
import jax
import jax.numpy as jnp
from jax import lax
from jax.sharding import PartitionSpec as P

beta_momentum = 0.9
eps_norm = 1e-06


def shards(local_grads, left_root, right_root, accumulator, momentum, block_owner, block_slot):
    data_count = lax.axis_size("dp")
    model_count = lax.axis_size("mp")
    model_here = lax.axis_index("mp")
    block_count = local_grads.shape[1]
    width = local_grads.shape[2]
    piece_rows = width // data_count
    grad_sum = lax.psum_scatter(
        local_grads[0].astype(jnp.float32).astype(jnp.bfloat16),
        "dp",
        scatter_dimension=1,
        tiled=True,
    ).astype(jnp.float32)
    accum_new = accumulator + grad_sum * grad_sum
    adagrad = grad_sum * lax.rsqrt(accum_new)
    ada_square = jnp.sum(adagrad * adagrad, axis=(1, 2))
    grad_round = grad_sum.astype(jnp.bfloat16)
    owner_table = block_owner.reshape(model_count, block_count)
    slot_table = block_slot.reshape(model_count, block_count)
    owner_home = lax.dynamic_index_in_dim(owner_table, model_here, 0, keepdims=False)
    model_ids = jnp.arange(model_count, dtype=jnp.int32)
    onehot_home = (owner_home[None, :] == model_ids[:, None]).astype(jnp.bfloat16)
    outgoing = jnp.einsum(
        "oj,jrb->orb", onehot_home, grad_round, preferred_element_type=jnp.float32
    ).astype(jnp.bfloat16)
    received_rows = lax.all_to_all(outgoing, "mp", split_axis=0, concat_axis=0, tiled=True)
    owned_here = owner_table == model_here
    slot_ids = jnp.arange(data_count, dtype=jnp.int32)
    matches = owned_here[None, :, :] & (slot_table[None, :, :] == slot_ids[:, None, None])
    selector_wide = jnp.sum(matches.astype(jnp.float32), axis=2)
    selection_matrix = selector_wide.astype(jnp.bfloat16)
    indexed_by_slot = jnp.einsum(
        "oj,jhw->ohw", selection_matrix, received_rows, preferred_element_type=jnp.float32
    ).astype(jnp.bfloat16)
    left_factor = left_root[0, 0]
    right_factor = right_root[0, 0]
    half_product = jnp.einsum(
        "krb,bc->krc",
        lax.all_to_all(indexed_by_slot, "dp", split_axis=0, concat_axis=0, tiled=True),
        right_factor,
        preferred_element_type=jnp.float32,
    ).astype(jnp.bfloat16)
    half_full = half_product.reshape(width, width)
    precond = jnp.dot(left_factor, half_full, preferred_element_type=jnp.float32).astype(
        jnp.bfloat16
    )
    precond_rows = precond.reshape(data_count, piece_rows, width)
    returned_rows = lax.all_to_all(precond_rows, "dp", split_axis=0, concat_axis=0, tiled=True)
    home_rows = jnp.einsum(
        "ao,afw->ofw", selection_matrix, returned_rows, preferred_element_type=jnp.float32
    ).astype(jnp.bfloat16)
    gathered_rows = lax.all_to_all(home_rows, "mp", split_axis=0, concat_axis=0, tiled=True)
    precond_home = jnp.einsum(
        "oj,orb->jrb", onehot_home, gathered_rows, preferred_element_type=jnp.float32
    )
    pre_square = jnp.sum(precond_home * precond_home, axis=(1, 2))
    adagrad_grand_total, pre_total = lax.psum((ada_square, pre_square), "dp")
    graft_scale = jnp.sqrt(adagrad_grand_total / (pre_total + eps_norm))
    momentum_new = (
        beta_momentum * momentum.astype(jnp.float32) + precond_home * graft_scale[:, None, None]
    )
    update_part = momentum_new.astype(jnp.bfloat16)
    update = lax.all_gather(update_part, "dp", axis=1, tiled=True)
    return (accum_new, update)


def solution(mesh):
    placed = (
        P("dp", "mp", None, None),
        P("mp", "dp", None, None),
        P("mp", "dp", None, None),
        P("mp", "dp", None),
        P("mp", "dp", None),
        P(),
        P(),
    )
    return jax.shard_map(
        shards,
        mesh=mesh,
        in_specs=placed,
        out_specs=(P("mp", "dp", None), P("mp", None, None)),
        check_vma=False,
    )
```

profile of v0, /device:TPU:1, one launch (start us, length us, event | category | flops | bytes accessed | tf_op | source)
XLA Modules:
  0.0 372.9 jit_solution(2600381001811587538)
XLA Ops:
  7.2 0.0 copy-start
  7.2 0.0 reduce-scatter.2.cloned.1.call-start
  7.2 0.0 copy-start.4
  7.2 0.7 reduce-scatter.2.cloned.1.call-update
  7.9 0.1 copy-done.4
  8.0 0.1 reshape.20
  8.1 57.4 %reduce-scatter.2.cloned.1.call-done = bf16[4,128,1024]{2,1,0:T(8,128)(2,1)} async-done(((bf16[4,1024,1024]{2,1,0:T(8,128)(2,1)}), bf16[4,128,1024]{2,1,0:T(8,128)(2,1)}) %reduce-scatter.2.cloned.1.call-update) | async-done | bytes 1048592 | tf_op jit(solution)/shard_map/reduce_scatter | solution.py:17
  65.5 2.6 convolution_convert_fusion.1
  68.2 4.3 %copy.33 = bf16[16,128,1024]{2,1,0:T(8,128)(2,1)} copy(bf16[16,128,1024]{2,0,1:T(8,128)(2,1)S(1)} %convolution_convert_fusion.1) | data formatting | bytes 8388608 | tf_op jit(solution)/shard_map/convert_element_type | solution.py:34
  72.5 6.8 %all-to-all-start = ((bf16[16,128,1024]{2,1,0:T(8,128)(2,1)}), bf16[16,128,1024]{2,1,0:T(8,128)(2,1)}, u32[]{:S(2)}, u32[]{:S(2)}) async-start(bf16[16,128,1024]{2,1,0:T(8,128)(2,1)} %copy.33), calls=%async_computation.1 | async-start | bytes 8388608 | tf_op jit(solution)/shard_map/all_to_all | solution.py:35
  79.4 0.1 copy.30
  79.5 0.1 eq.46
  79.6 0.1 copy.31
  79.7 60.3 %all-to-all-done = bf16[16,128,1024]{2,1,0:T(8,128)(2,1)} async-done(((bf16[16,128,1024]{2,1,0:T(8,128)(2,1)}), bf16[16,128,1024]{2,1,0:T(8,128)(2,1)}, u32[]{:S(2)}, u32[]{:S(2)}) %all-to-all-start) | async-done | bytes 4194336 | tf_op jit(solution)/shard_map/all_to_all | solution.py:35
  140.0 4.6 %fusion.18 = bf16[8,128,1024]{2,0,1:T(8,128)(2,1)S(1)} fusion(bf16[16,128,1024]{2,1,0:T(8,128)(2,1)} %all-to-all-done, bf16[8,16]{1,0:T(8,128)(2,1)S(1)} %convert_reduce_fusion), kind=kOutput, calls=%fused_computation.20 | convolution fusion | flops 34603008 | bytes 6291712 | tf_op jit(solution)/shard_map/oj,jhw->ohw/dot_general | solution.py:41
  144.6 1.2 copy.35
  145.7 35.5 %all_to_all.20 = bf16[8,128,1024]{2,1,0:T(8,128)(2,1)S(1)} all-to-all(bf16[8,128,1024]{2,1,0:T(8,128)(2,1)S(1)} %copy.35), channel_id=1, replica_groups=mesh['dp'=8,'mp'=16] {'dp'}, dimensions={0} | all-to-all | bytes 4194304 | tf_op jit(solution)/shard_map/all_to_all | solution.py:48
  181.3 2.3 fusion.15
  183.6 2.3 fusion.12
  186.0 30.0 %all_to_all.21 = bf16[8,128,1024]{2,1,0:T(8,128)(2,1)S(1)} all-to-all(bf16[8,128,1024]{2,1,0:T(8,128)(2,1)S(1)} %bitcast.33), channel_id=1, replica_groups=mesh['dp'=8,'mp'=16] {'dp'}, dimensions={0} | all-to-all | bytes 4194304 | tf_op jit(solution)/shard_map/all_to_all | solution.py:57
  215.9 1.6 convolution_convert_fusion
  217.6 4.3 %copy.37 = bf16[16,128,1024]{2,1,0:T(8,128)(2,1)} copy(bf16[16,128,1024]{2,0,1:T(8,128)(2,1)S(1)} %convolution_convert_fusion) | data formatting | bytes 8388608 | tf_op jit(solution)/shard_map/convert_element_type | solution.py:60
  221.9 4.7 %all-to-all-start.3 = ((bf16[16,128,1024]{2,1,0:T(8,128)(2,1)}), bf16[16,128,1024]{2,1,0:T(8,128)(2,1)}, u32[]{:S(2)}, u32[]{:S(2)}) async-start(bf16[16,128,1024]{2,1,0:T(8,128)(2,1)} %copy.37), calls=%async_computation.4 | async-start | bytes 8388608 | tf_op jit(solution)/shard_map/all_to_all | solution.py:61
  226.6 0.0 all-gather.2.cloned.1.call-start
  226.6 3.4 fusion.6
  230.0 58.6 %all-to-all-done.3 = bf16[16,128,1024]{2,1,0:T(8,128)(2,1)} async-done(((bf16[16,128,1024]{2,1,0:T(8,128)(2,1)}), bf16[16,128,1024]{2,1,0:T(8,128)(2,1)}, u32[]{:S(2)}, u32[]{:S(2)}) %all-to-all-start.3) | async-done | bytes 4194336 | tf_op jit(solution)/shard_map/all_to_all | solution.py:61
  288.6 5.0 %multiply_reduce_fusion = (f32[4]{0:T(128)S(1)}, f32[4,128,1024]{2,0,1:T(4,128)S(1)}) fusion(bf16[16,128,1024]{2,1,0:T(8,128)(2,1)} %all-to-all-done.3, s32[4]{0:T(128)S(1)} %dynamic-slice_bitcast_fusion), kind=kOutput, calls=%fused_computation.17 | convolution fusion | flops 17825852 | bytes 6291488 | tf_op jit(solution)/shard_map/oj,orb->jrb/dot_general | solution.py:62
  293.6 13.7 %all-reduce = (f32[4]{0:T(128)S(1)}, f32[4]{0:T(128)S(1)}) all-reduce(f32[4]{0:T(128)S(1)} %get-tuple-element.14, f32[4]{0:T(128)S(1)} %get-tuple-element.16), channel_id=1, replica_groups=mesh['dp'=8,'mp'=16] {'dp'}, use_global_device_ids=true, to_apply=%region_3.4 | all-reduce | flops 8 | bytes 64 | tf_op jit(solution)/shard_map/psum | solution.py:66
  307.3 2.2 add_convert_fusion
  309.5 0.0 all-gather.2.cloned.1.call-update
  309.5 46.7 %all-gather.2.cloned.1.call-done = bf16[4,1024,1024]{2,0,1:T(4,128)(2,1)} async-done(((bf16[4,128,1024]{2,0,1:T(4,128)(2,1)}), bf16[4,1024,1024]{2,0,1:T(4,128)(2,1)}) %all-gather.2.cloned.1.call-update) | async-done | bytes 8388624 | tf_op jit(solution)/shard_map/all_gather | solution.py:72
  356.2 9.8 %copy.39 = bf16[4,1024,1024]{2,1,0:T(8,128)(2,1)} copy(bf16[4,1024,1024]{2,0,1:T(4,128)(2,1)} %all-gather.2.cloned.1.call-done) | data formatting | bytes 16777216
  (15 shorter events, 0.1 us)
Async XLA Ops:
  7.2 174.1 %copy-start = (bf16[1,1,1024,1024]{3,2,1,0:T(8,128)(2,1)S(1)}, bf16[1,1,1024,1024]{3,2,1,0:T(8,128)(2,1)}, u32[]{:S(2)}) copy-start(bf16[1,1,1024,1024]{3,2,1,0:T(8,128)(2,1)} %param.9) | copy-start | bytes 6291460
  7.2 58.4 %reduce-scatter.2.cloned.1.call-start = ((), (), s32[]{:S(2)}) async-start(), calls=%async_computation.5 | async-start | bytes 9437184 | tf_op jit(solution)/shard_map/reduce_scatter | solution.py:17
  7.2 0.8 copy-start.4
  72.5 7.0 %copy-start.5 = (s32[64]{0:T(128)S(1)}, s32[64]{0:T(128)}, u32[]{:S(2)}) copy-start(s32[64]{0:T(128)} %param.13) | copy-start | bytes 772
  72.5 67.5 %all-to-all-start = ((bf16[16,128,1024]{2,1,0:T(8,128)(2,1)}), bf16[16,128,1024]{2,1,0:T(8,128)(2,1)}, u32[]{:S(2)}, u32[]{:S(2)}) async-start(bf16[16,128,1024]{2,1,0:T(8,128)(2,1)} %copy.33), calls=%async_computation.1 | async-start | bytes 8388608 | tf_op jit(solution)/shard_map/all_to_all | solution.py:35
  181.3 2.4 copy-start.6
  221.9 4.7 %copy-start.2 = (bf16[4,128,1024]{2,1,0:T(8,128)(2,1)S(1)}, bf16[4,128,1024]{2,1,0:T(8,128)(2,1)}, u32[]{:S(2)}) copy-start(bf16[4,128,1024]{2,1,0:T(8,128)(2,1)} %reduce-scatter.2.cloned.1.call-done) | copy-start | bytes 3145732
  221.9 66.7 %all-to-all-start.3 = ((bf16[16,128,1024]{2,1,0:T(8,128)(2,1)}), bf16[16,128,1024]{2,1,0:T(8,128)(2,1)}, u32[]{:S(2)}, u32[]{:S(2)}) async-start(bf16[16,128,1024]{2,1,0:T(8,128)(2,1)} %copy.37), calls=%async_computation.4 | async-start | bytes 8388608 | tf_op jit(solution)/shard_map/all_to_all | solution.py:61
  226.6 129.7 %all-gather.2.cloned.1.call-start = ((), (), s32[]{:S(2)}) async-start(), calls=%async_computation.6 | async-start | bytes 9437184 | tf_op jit(solution)/shard_map/all_gather | solution.py:72
  230.0 77.3 %copy-start.3 = (bf16[4,128,1024]{2,1,0:T(8,128)(2,1)S(1)}, bf16[4,128,1024]{2,1,0:T(8,128)(2,1)}, u32[]{:S(2)}) copy-start(bf16[4,128,1024]{2,1,0:T(8,128)(2,1)} %param.11) | copy-start | bytes 3145732
  356.2 9.8 %copy-start.1 = (bf16[1,1,1024,1024]{3,2,1,0:T(8,128)(2,1)S(1)}, bf16[1,1,1024,1024]{3,2,1,0:T(8,128)(2,1)}, u32[]{:S(2)}) copy-start(bf16[1,1,1024,1024]{3,2,1,0:T(8,128)(2,1)} %param.9) | copy-start | bytes 6291460
Sparse Core Ops, SparseCore 0:
  10.4 55.0 reduce-scatter.1
  309.7 46.5 all-gather.1
where the time goes:
time: 373 us
  waiting for transfers between devices  224 us (60%)
  blocking collectives  79.2 us (21%)
  local copies, waits for them, and re-layouts  20.1 us (5%)
  matrix products  18.5 us (5%)
  between operations  14.2 us (4%)
  starting transfers between devices  11.6 us (3%)
  other arithmetic  5.65 us (2%)
    all_to_all x1, waiting for transfers between devices, shards(): lax.all_to_all(outgoing, 'mp', split_axis=0, concat_axis=0, tiled=True)  60.3 us
    all_to_all x1, waiting for transfers between devices, shards(): lax.all_to_all(home_rows, 'mp', split_axis=0, concat_axis=0, tiled=True)  58.6 us
    reduce_scatter x1, waiting for transfers between devices, shards(): lax.psum_scatter(local_grads[0].astype(jnp.float32).astype(jnp.bfloat16),...  57.4 us
    all_gather x1, waiting for transfers between devices, shards(): update = lax.all_gather(update_part, 'dp', axis=1, tiled=True)  46.7 us
    all_to_all x1, blocking collectives, shards(): lax.all_to_all(indexed_by_slot, 'dp', split_axis=0, concat_axis=0, tiled=...  35.5 us
    all_to_all x1, blocking collectives, shards(): lax.all_to_all(precond_rows, 'dp', split_axis=0, concat_axis=0, tiled=True)  30 us
    psum x1, blocking collectives, shards(): adagrad_grand_total, pre_total = lax.psum((ada_square, pre_square), 'dp')  13.7 us
    unnamed x15, local copies, waits for them, and re-layouts  9.92 us
  transfers between devices with their start and end apart: 4, of which 4 were waited for; matrix products, arithmetic and copies ran while one was open for 1% of the time, Pallas kernels for 0%

commit v1 on v0

v1 whole, which is shorter than its diff:
```python
import jax
import jax.numpy as jnp
from jax import lax
from jax.experimental import pallas as pl
from jax.experimental.pallas import tpu as pltpu
from jax.sharding import PartitionSpec as P

MESH = pl.DeviceIdType.MESH
BF = jnp.bfloat16
F32 = jnp.float32
beta_momentum = 0.9
eps_norm = 1e-06

CHUNKS = 4
ROWS = 32
W = 1024
COLUMN = ((1, 0), (3, 0), (2, 0), (1, 1), (3, 1), (2, 1), (0, 1))


def kernel(
    inv, loc, g, left, right, acc, mom, out_acc, out_upd,
    own, sib, t1p, t1m, t2p, t2m, accv, momv, lv, rv, ada, ar, sbuf, qb, p1, vb, gb, half, pp,
    nrm, nv, nt, nw, v2, wb, wp, hh, scl, up,
    s_own, s_in, s_sib, s_t1, s_t2, s_fa, s_fb, s_fc, s_ra, s_rb, s_rc, s_sm,
    s_a1, s_a2, s_sb, s_out, snd,
):
    dp = lax.axis_index("dp")
    mp = lax.axis_index("mp")
    y, c = dp // 2, dp % 2
    z, x = mp // 4, mp % 4
    piece_a, piece_h = mp // 8, mp % 8

    def col(dy, dc):
        return ((y + dy) % 4) * 2 + (c + dc) % 2

    def plane(k):
        return ((z + k // 4) % 4) * 4 + (x + k % 4) % 4

    def put(src, dst, ssem, rsem, device):
        pltpu.make_async_remote_copy(
            src_ref=src, dst_ref=dst, send_sem=snd.at[ssem], recv_sem=rsem,
            device_id=device, device_id_type=MESH,
        ).start()

    def keep(src, dst, sem):
        pltpu.make_async_copy(src, dst, sem).start()

    def await_bytes(ref, sem):
        pltpu.make_async_copy(ref, ref, sem).wait()

    def each_in_plane(body):
        def step(k, carry):
            body(plane(k))
            return carry

        lax.fori_loop(1, 16, step, 0)

    def piece(m):
        return pl.ds(pl.multiple_of((m // 8) * 16, 16), 16), pl.ds(
            pl.multiple_of((m % 8) * 128, 128), 128
        )

    up_dev = (col(1, 0), mp)
    down_dev = (col(3, 0), mp)
    sib_dev = (col(0, 1), mp)
    targets = ((y + 2) % 4, (y + 1) % 4, (y + 3) % 4, y)

    for q in range(CHUNKS):
        for k in range(4):
            keep(
                g.at[:, targets[k], c, pl.ds(q * ROWS, ROWS), :],
                own.at[q, targets[k]],
                s_own.at[q * 4 + k],
            )
    keep(acc, accv, s_in.at[0])
    keep(right, rv, s_in.at[1])
    keep(left, lv, s_in.at[2])
    keep(mom, momv, s_in.at[3])

    barrier = pltpu.get_barrier_semaphore()

    def greet(m):
        pl.semaphore_signal(barrier, inc=1, device_id=(dp, m), device_id_type=MESH)

    for dy, dc in COLUMN:
        pl.semaphore_signal(barrier, inc=1, device_id=(col(dy, dc), mp), device_id_type=MESH)
    each_in_plane(greet)
    pl.semaphore_wait(barrier, 22)

    for q in range(CHUNKS):
        for k in range(4):
            put(
                g.at[:, targets[k], 1 - c, pl.ds(q * ROWS, ROWS), :],
                sib.at[q, targets[k]],
                0,
                s_sib.at[q * 4 + k],
                sib_dev,
            )

    for j in range(4):
        ada[j] = jnp.zeros((8, 128), F32)

    def both(q, k, j):
        t = targets[k]
        return own[q, t, j].astype(F32) + sib[q, t, j].astype(F32)

    def arrived(q, k):
        await_bytes(own.at[q, targets[k]], s_own.at[q * 4 + k])
        await_bytes(sib.at[q, targets[k]], s_sib.at[q * 4 + k])

    def fold(v):
        rows, lanes = v.shape
        v = jnp.sum(v.reshape(rows // 8, 8, lanes), axis=0)
        total = v[:, 0:128]
        for i in range(1, lanes // 128):
            total = total + v[:, i * 128 : (i + 1) * 128]
        return total

    def f0(q):
        arrived(q, 0)
        t = targets[0]
        for j in range(4):
            own[q, t, j] = both(q, 0, j).astype(BF)
        put(own.at[q, t, pl.ds(0, 2)], t1p.at[q], 1, s_t1.at[q * 2], up_dev)
        put(own.at[q, t, pl.ds(2, 2)], t1m.at[q], 1, s_t1.at[q * 2 + 1], down_dev)

    def f1(q):
        arrived(q, 1)
        arrived(q, 2)
        await_bytes(t1p.at[q], s_t1.at[q * 2])
        await_bytes(t1m.at[q], s_t1.at[q * 2 + 1])
        for j in range(4):
            value = both(q, 1, j)
            if j < 2:
                value = value + t1p[q, j].astype(F32)
            own[q, targets[1], j] = value.astype(BF)
        put(own.at[q, targets[1]], t2p.at[q], 2, s_t2.at[q * 2], up_dev)
        for j in range(4):
            value = both(q, 2, j)
            if j >= 2:
                value = value + t1m[q, j - 2].astype(F32)
            own[q, targets[2], j] = value.astype(BF)
        put(own.at[q, targets[2]], t2m.at[q], 2, s_t2.at[q * 2 + 1], down_dev)

    def f2(q):
        arrived(q, 3)
        await_bytes(t2p.at[q], s_t2.at[q * 2])
        await_bytes(t2m.at[q], s_t2.at[q * 2 + 1])
        if q == 0:
            await_bytes(accv, s_in.at[0])
        rows = pl.ds(q * ROWS, ROWS)
        for j in range(4):
            total = both(q, 3, j) + t2p[q, j].astype(F32) + t2m[q, j].astype(F32)
            fresh = accv[j, rows, :] + total * total
            accv[j, rows, :] = fresh
            step = total * lax.rsqrt(fresh)
            ada[j] += fold(step * step)
            sbuf[q, j] = total.astype(BF)
        keep(accv.at[:, rows, :], out_acc.at[:, rows, :], s_out.at[q])

        def spread(m):
            r, l = piece(m)
            put(sbuf.at[q, :, r, l], qb[q].at[pl.ds(mp * 4, 4)], 3, s_fa.at[q], (dp, m))

        each_in_plane(spread)
        r, l = piece(mp)
        keep(sbuf.at[q, :, r, l], qb[q].at[pl.ds(mp * 4, 4)], s_fa.at[q])

    def share_adagrad():
        ar[dp] = ada[...]
        for dy, dc in COLUMN:
            put(ada, ar.at[dp], 4, s_sm.at[0], (col(dy, dc), mp))

    def f3(q):
        await_bytes(qb[q], s_fa.at[q])

        def pick(i, carry):
            for n in range(8):
                p1[q, i * 8 + n] = qb[q][inv[i * 8 + n]]
            return carry

        lax.fori_loop(0, 16, pick, 0)
        r, l = piece(mp)

        def deal(o):
            put(p1.at[q, pl.ds(o * 8, 8)], vb.at[q, :, r, l], 5, s_fb.at[q], (dp, o))

        each_in_plane(deal)
        keep(p1.at[q, pl.ds(mp * 8, 8)], vb.at[q, :, r, l], s_fb.at[q])

    def f4(q):
        await_bytes(vb.at[q], s_fb.at[q])
        for dy, dc in COLUMN:
            s = col(dy, dc)
            put(vb.at[q, s], gb.at[q, dp], 6, s_fc.at[q], (s, mp))
        keep(vb.at[q, dp], gb.at[q, dp], s_fc.at[q])

    def f5(q):
        if q == 0:
            await_bytes(rv, s_in.at[1])
        await_bytes(gb.at[q], s_fc.at[q])

        def tile(n, carry):
            lanes = pl.ds(pl.multiple_of(n * 256, 256), 256)
            rows = gb[q].reshape(8 * ROWS, W)
            value = jnp.dot(rows, rv[:, lanes], preferred_element_type=F32)
            half[:, pl.ds(q * ROWS, ROWS), lanes] = value.astype(BF).reshape(8, ROWS, 256)
            return carry

        lax.fori_loop(0, 4, tile, 0)

    def r0(q):
        if q == 0:
            await_bytes(lv, s_in.at[2])
            nrm[...] = jnp.zeros((8, 128), F32)

        def tile(n, carry):
            lanes = pl.ds(pl.multiple_of(n * 256, 256), 256)
            rows = lv[:, pl.ds(q * ROWS, ROWS), :].reshape(8 * ROWS, W)
            value = jnp.dot(rows, half[:, :, lanes].reshape(W, 256), preferred_element_type=F32)
            value = value.astype(BF)
            pp[q, :, :, lanes] = value.reshape(8, ROWS, 256)
            wide = value.astype(F32)
            nrm[...] += fold(wide * wide)
            return carry

        lax.fori_loop(0, 4, tile, 0)
        for dy, dc in COLUMN:
            d = col(dy, dc)
            put(pp.at[q, d], v2.at[q, dp], 7, s_ra.at[q], (d, mp))
        keep(pp.at[q, dp], v2.at[q, dp], s_ra.at[q])

    def share_norm():
        total = jnp.full((8, 128), jnp.sum(nrm[...]), F32)
        nrm[...] = total
        nv[dp] = total
        for dy, dc in COLUMN:
            put(nrm, nv.at[dp], 8, s_sm.at[1], (col(dy, dc), mp))

    def spread_norms():
        await_bytes(nv.at[pl.ds(0, 7)], s_sm.at[1])
        row = lax.broadcasted_iota(jnp.int32, (8, 128), 0)
        table = jnp.zeros((8, 128), F32)
        for s in range(8):
            table = jnp.where(row == s, nv[s], table)
        nt[...] = table
        nw[mp] = table

        def send(m):
            put(nt, nw.at[mp], 9, s_sm.at[2], (dp, m))

        each_in_plane(send)

    def r1(q):
        await_bytes(v2.at[q], s_ra.at[q])

        def spread(m):
            r, l = piece(m)
            put(v2.at[q, :, r, l], wb[q].at[pl.ds(mp * 8, 8)], 10, s_rb.at[q], (dp, m))

        each_in_plane(spread)
        r, l = piece(mp)
        keep(v2.at[q, :, r, l], wb[q].at[pl.ds(mp * 8, 8)], s_rb.at[q])

    def r2(q):
        await_bytes(wb[q], s_rb.at[q])

        def pick(i, carry):
            for n in range(8):
                wp[q, i * 8 + n] = wb[q][loc[i * 8 + n]]
            return carry

        lax.fori_loop(0, 8, pick, 0)
        r, l = piece(mp)

        def deal(m):
            put(wp.at[q, pl.ds(m * 4, 4)], hh.at[q, :, r, l], 11, s_rc.at[q], (dp, m))

        each_in_plane(deal)
        keep(wp.at[q, pl.ds(mp * 4, 4)], hh.at[q, :, r, l], s_rc.at[q])

    def scales():
        await_bytes(ar.at[pl.ds(0, 7)], s_sm.at[0])
        await_bytes(nw.at[pl.ds(0, 15)], s_sm.at[2])
        await_bytes(momv, s_in.at[3])
        row = lax.broadcasted_iota(jnp.int32, (8, 128), 0)
        for j in range(4):
            place = loc[mp * 4 + j]
            mine = nw[place // 8]
            pre = jnp.sum(jnp.where(row == place % 8, mine, 0.0), axis=0, keepdims=True)
            ada_total = jnp.sum(ar[:, j])
            scl[j] = jnp.broadcast_to(jnp.sqrt(ada_total / (pre + eps_norm)), (8, 128))

    def group(dy):
        return col(dy, 0)

    def rows_of(dy, q, blocks=None):
        if blocks is None:
            return out_upd.at[:, group(dy), pl.ds(q * ROWS, ROWS), :]
        return out_upd.at[pl.ds(blocks, 2), group(dy), pl.ds(q * ROWS, ROWS), :]

    def r3(q):
        await_bytes(hh.at[q], s_rc.at[q])
        for j in range(4):
            scale = jnp.concatenate([scl[j, 0:1, :]] * 8, axis=1)
            value = (
                beta_momentum * momv[j, pl.ds(q * ROWS, ROWS), :].astype(F32)
                + scale * hh[q, j].astype(F32)
            )
            up[q, j] = value.astype(BF)
        put(up.at[q], rows_of(0, q), 12, s_a1.at[q * 2], up_dev)
        put(up.at[q], rows_of(0, q), 12, s_a1.at[q * 2 + 1], down_dev)
        put(up.at[q], rows_of(0, q), 14, s_sb.at[q * 4], sib_dev)
        keep(up.at[q], rows_of(0, q), s_out.at[4 + q])

    def r4(q):
        await_bytes(rows_of(3, q), s_a1.at[q * 2])
        put(rows_of(3, q, 0), rows_of(3, q, 0), 13, s_a2.at[q * 2], up_dev)
        put(rows_of(3, q), rows_of(3, q), 14, s_sb.at[q * 4 + 1], sib_dev)
        await_bytes(rows_of(1, q), s_a1.at[q * 2 + 1])
        put(rows_of(1, q, 2), rows_of(1, q, 2), 13, s_a2.at[q * 2 + 1], down_dev)
        put(rows_of(1, q), rows_of(1, q), 14, s_sb.at[q * 4 + 2], sib_dev)

    def r5(q):
        await_bytes(rows_of(2, q, 0), s_a2.at[q * 2])
        await_bytes(rows_of(2, q, 2), s_a2.at[q * 2 + 1])
        put(rows_of(2, q), rows_of(2, q), 14, s_sb.at[q * 4 + 3], sib_dev)

    forward = (f0, f1, f2, f3, f4, f5)
    for t in range(CHUNKS + len(forward) - 1):
        for n, stage in enumerate(forward):
            if 0 <= t - n < CHUNKS:
                stage(t - n)
        if t == CHUNKS + 1:
            share_adagrad()
    for q in range(CHUNKS):
        r0(q)
    share_norm()
    back = (r1, r2, r3, r4, r5)
    for t in range(CHUNKS + len(back) - 1):
        if t == 1:
            spread_norms()
        if t == 2:
            scales()
        for n, stage in enumerate(back):
            if 0 <= t - n < CHUNKS:
                stage(t - n)

    for q in range(CHUNKS):
        for k in range(4):
            await_bytes(rows_of((0, 3, 1, 2)[k], q), s_sb.at[q * 4 + k])
        rows = pl.ds(q * ROWS, ROWS)
        await_bytes(out_acc.at[:, rows, :], s_out.at[q])
        await_bytes(rows_of(0, q), s_out.at[4 + q])
        for k in range(4):
            await_bytes(sib.at[q, k], snd.at[0])
            await_bytes(rows_of(k, q), snd.at[14])
        await_bytes(t1p.at[q], snd.at[1])
        await_bytes(t1m.at[q], snd.at[1])
        await_bytes(t2p.at[q], snd.at[2])
        await_bytes(t2m.at[q], snd.at[2])
        await_bytes(qb[q].at[pl.ds(0, 60)], snd.at[3])
        await_bytes(p1.at[q, pl.ds(0, 120)], snd.at[5])
        await_bytes(vb.at[q, pl.ds(0, 7)], snd.at[6])
        await_bytes(pp.at[q, pl.ds(0, 7)], snd.at[7])
        await_bytes(wb[q].at[pl.ds(0, 120)], snd.at[10])
        await_bytes(wp.at[q, pl.ds(0, 60)], snd.at[11])
        await_bytes(rows_of(1, q), snd.at[12])
        await_bytes(rows_of(3, q), snd.at[12])
        await_bytes(rows_of(2, q), snd.at[13])
    await_bytes(ar.at[pl.ds(0, 7)], snd.at[4])
    await_bytes(nv.at[pl.ds(0, 7)], snd.at[8])
    await_bytes(nw.at[pl.ds(0, 15)], snd.at[9])


def shards(local_grads, left_root, right_root, accumulator, momentum, block_owner, block_slot):
    place = block_owner * 8 + block_slot
    hit = place[None, :] == jnp.arange(128, dtype=jnp.int32)[:, None]
    inverse = jnp.sum(
        jnp.where(hit, jnp.arange(64, dtype=jnp.int32)[None, :], 0), axis=1, dtype=jnp.int32
    )
    hbm = pl.BlockSpec(memory_space=pl.ANY)
    smem = pl.BlockSpec(memory_space=pltpu.SMEM)
    V = pltpu.VMEM
    dma = pltpu.SemaphoreType.DMA
    C, R = CHUNKS, ROWS
    scratch = [
        V((C, 4, 4, R, W), BF), V((C, 4, 4, R, W), BF),
        V((C, 2, R, W), BF), V((C, 2, R, W), BF),
        V((C, 4, R, W), BF), V((C, 4, R, W), BF),
        V((4, 128, W), F32), V((4, 128, W), BF),
        V((8, 128, W), BF), V((W, W), BF),
        V((4, 8, 128), F32), V((8, 4, 8, 128), F32),
        V((C, 4, R, W), BF),
        [V((64, 16, 128), BF)] * C, V((C, 128, 16, 128), BF),
        V((C, 8, R, W), BF), V((C, 8, R, W), BF),
        V((8, 128, W), BF), V((C, 8, R, W), BF),
        V((8, 128), F32), V((8, 8, 128), F32),
        V((8, 128), F32), V((16, 8, 128), F32),
        V((C, 8, R, W), BF),
        [V((128, 16, 128), BF)] * C, V((C, 64, 16, 128), BF),
        V((C, 4, R, W), BF), V((4, 8, 128), F32), V((C, 4, R, W), BF),
        dma((16,)), dma((4,)), dma((16,)), dma((8,)), dma((8,)),
        dma((4,)), dma((4,)), dma((4,)), dma((4,)), dma((4,)), dma((4,)),
        dma((3,)), dma((8,)), dma((8,)), dma((16,)), dma((8,)), dma((15,)),
    ]
    accum_new, update = pl.pallas_call(
        kernel,
        out_shape=(
            jax.ShapeDtypeStruct((4, 128, W), F32),
            jax.ShapeDtypeStruct((4, 8, 128, W), BF),
        ),
        in_specs=[smem, smem] + [hbm] * 5,
        out_specs=(hbm, hbm),
        scratch_shapes=scratch,
        name="shampoo_step",
        compiler_params=pltpu.CompilerParams(
            collective_id=0, has_side_effects=True, vmem_limit_bytes=56 * 2**20
        ),
    )(
        inverse,
        place,
        local_grads.reshape(4, 4, 2, 128, W),
        left_root.reshape(8, 128, W),
        right_root.reshape(W, W),
        accumulator,
        momentum,
    )
    return accum_new, update.reshape(4, W, W)


def solution(mesh):
    placed = (
        P("dp", "mp", None, None),
        P("mp", "dp", None, None),
        P("mp", "dp", None, None),
        P("mp", "dp", None),
        P("mp", "dp", None),
        P(),
        P(),
    )
    return jax.shard_map(
        shards,
        mesh=mesh,
        in_specs=placed,
        out_specs=(P("mp", "dp", None), P("mp", None, None)),
        check_vma=False,
    )
```

time: 373 us -> 173 us (0.46)
  waiting for transfers between devices: 224 us -> 0 us
  Pallas kernels: 0 us -> 160 us
  blocking collectives: 79.2 us -> 0 us
  matrix products: 18.5 us -> 0 us
  between operations: 14.2 us -> 0.64 us
  starting transfers between devices: 11.6 us -> 0 us
  local copies, waits for them, and re-layouts: 20.1 us -> 10.9 us
  other arithmetic: 5.65 us -> 1.28 us
    pallas_call x0 -> x1, Pallas kernels: none -> 160 us  [shards(): pl.pallas_call(kernel, out_shape=(jax.ShapeDtypeStruct((4, 128, W), F32),...]
    all_to_all x2 -> x0, waiting for transfers between devices: 119 us -> none  [the longest x1 60.3 us: shards(): lax.all_to_all(outgoing, 'mp', split_axis=0, concat_axis=0, tiled=True)]
    all_to_all x2 -> x0, blocking collectives: 65.5 us -> none  [the longest x1 35.5 us: shards(): lax.all_to_all(indexed_by_slot, 'dp', split_axis=0, concat_axis=0, tiled=...]
    reduce_scatter x1 -> x0, waiting for transfers between devices: 57.4 us -> none  [shards(): lax.psum_scatter(local_grads[0].astype(jnp.float32).astype(jnp.bfloat16),...]
    all_gather x1 -> x0, waiting for transfers between devices: 46.7 us -> none  [shards(): update = lax.all_gather(update_part, 'dp', axis=1, tiled=True)]
    dot_general x6 -> x0, matrix products: 18.5 us -> none  [the longest x1 4.99 us: shards(): jnp.einsum('oj,orb->jrb', onehot_home, gathered_rows, preferred_element_t...]
    psum x1 -> x0, blocking collectives: 13.7 us -> none  [shards(): adagrad_grand_total, pre_total = lax.psum((ada_square, pre_square), 'dp')]
    all_to_all x2 -> x0, starting transfers between devices: 11.5 us -> none  [the longest x1 6.85 us: shards(): lax.all_to_all(outgoing, 'mp', split_axis=0, concat_axis=0, tiled=True)]
  transfers between devices with their start and end apart: 4 -> 0, of which waited for: 4 -> 0; matrix products, arithmetic and copies ran while one was open for 1% -> 0% of each run, Pallas kernels for 0% -> 0%
where the time goes in v1:
time: 173 us; the launch traced here: 172 us
  Pallas kernels  160 us (92%)
  local copies, waits for them, and re-layouts  10.9 us (6%)
    pallas_call x1, Pallas kernels, shards(): pl.pallas_call(kernel, out_shape=(jax.ShapeDtypeStruct((4, 128, W), F32),...  160 us
    unnamed x4, local copies, waits for them, and re-layouts  10.9 us

profile of v1, /device:TPU:1, one launch (start us, length us, event | category | flops | bytes accessed | tf_op | source)
XLA Modules:
  0.0 172.4 jit_solution(16540582932358947792)
XLA Ops:
  0.6 0.7 multiply_add_fusion.loc
  1.3 0.0 copy-start
  1.3 0.6 select_reduce_fusion.inv
  1.9 0.0 copy-done
  1.9 159.6 %shampoo_step.1 = (f32[4,128,1024]{2,1,0:T(8,128)}, bf16[4,8,128,1024]{3,2,1,0:T(8,128)(2,1)}) custom-call(s32[128]{0:T(128)} %select_reduce_fusion.inv, s32[64]{0:T(128)} %copy-done, bf16[4,4,2,128,1024]{4,3,2,1,0:T(8,128)(2,1)} %bitcast.4, bf16[8,128,1024]{2,1,0:T(8,128)(2,1)} %bitcast.6, bf16[1024,1024]{1,0:T(8,128)(2,1)} %bitcast.7, ...), custom_call_target="tpu_custom_call" | custom-call | tf_op jit(solution)/shard_map/shampoo_step/pallas_call | solution.py:407
  161.5 3.2 %copy.11 = f32[4,128,1024]{2,1,0:T(8,128)} copy(f32[4,128,1024]{2,1,0:T(8,128)} %get-tuple-element.8) | data formatting | bytes 4194304
  164.7 7.8 %copy.12 = bf16[4,1024,1024]{2,1,0:T(8,128)(2,1)} copy(bf16[4,1024,1024]{2,1,0:T(8,128)(2,1)} %bitcast.5) | data formatting | bytes 16777216
Async XLA Ops:
  1.3 0.6 copy-start

commit v2 on v1

--- a/solution.py
+++ b/solution.py
@@ -14,15 +14,19 @@
 CHUNKS = 4
 ROWS = 32
 W = 1024
-COLUMN = ((1, 0), (3, 0), (2, 0), (1, 1), (3, 1), (2, 1), (0, 1))
+COLUMN = ((2, 0), (2, 1), (1, 0), (3, 0), (1, 1), (3, 1), (0, 1))
+PLANE = (
+    (2, 2), (1, 2), (2, 1), (3, 2), (2, 3), (0, 2), (2, 0), (1, 1),
+    (3, 3), (1, 3), (3, 1), (0, 1), (1, 0), (0, 3), (3, 0),
+)
 
 
 def kernel(
-    inv, loc, g, left, right, acc, mom, out_acc, out_upd,
+    owner, slot, g, left, right, acc, mom, out_acc, out_upd,
     own, sib, t1p, t1m, t2p, t2m, accv, momv, lv, rv, ada, ar, sbuf, qb, p1, vb, gb, half, pp,
-    nrm, nv, nt, nw, v2, wb, wp, hh, scl, up,
+    nrm, nv, nt, nw, v2, wb, wp, hh, scl, up, invv, inv,
     s_own, s_in, s_sib, s_t1, s_t2, s_fa, s_fb, s_fc, s_ra, s_rb, s_rc, s_sm,
-    s_a1, s_a2, s_sb, s_out, snd,
+    s_a1, s_a2, s_sb, s_out, s_inv, snd,
 ):
     dp = lax.axis_index("dp")
     mp = lax.axis_index("mp")
@@ -33,8 +37,8 @@
     def col(dy, dc):
         return ((y + dy) % 4) * 2 + (c + dc) % 2
 
-    def plane(k):
-        return ((z + k // 4) % 4) * 4 + (x + k % 4) % 4
+    def plane(dz, dx):
+        return ((z + dz) % 4) * 4 + (x + dx) % 4
 
     def put(src, dst, ssem, rsem, device):
         pltpu.make_async_remote_copy(
@@ -48,12 +52,14 @@
     def await_bytes(ref, sem):
         pltpu.make_async_copy(ref, ref, sem).wait()
 
+    ends = []
+
+    def place(b):
+        return owner[b] * 8 + slot[b]
+
     def each_in_plane(body):
-        def step(k, carry):
-            body(plane(k))
-            return carry
-
-        lax.fori_loop(1, 16, step, 0)
+        for dz, dx in PLANE:
+            body(plane(dz, dx))
 
     def piece(m):
         return pl.ds(pl.multiple_of((m // 8) * 16, 16), 16), pl.ds(
@@ -65,6 +71,14 @@
     sib_dev = (col(0, 1), mp)
     targets = ((y + 2) % 4, (y + 1) % 4, (y + 3) % 4, y)
 
+    barrier = pltpu.get_barrier_semaphore()
+
+    def greet(m):
+        pl.semaphore_signal(barrier, inc=1, device_id=(dp, m), device_id_type=MESH)
+
+    for dy, dc in COLUMN:
+        pl.semaphore_signal(barrier, inc=1, device_id=(col(dy, dc), mp), device_id_type=MESH)
+    each_in_plane(greet)
     for q in range(CHUNKS):
         for k in range(4):
             keep(
@@ -72,22 +86,21 @@
                 own.at[q, targets[k]],
                 s_own.at[q * 4 + k],
             )
+    lane = lax.broadcasted_iota(jnp.int32, (8, 128), 1)
+
+    def fill(b, table):
+        return jnp.where(lane == place(b), b, table)
+
+    invv[...] = lax.fori_loop(0, 64, fill, jnp.zeros((8, 128), jnp.int32))
+    keep(invv, inv, s_inv.at[0])
     keep(acc, accv, s_in.at[0])
     keep(right, rv, s_in.at[1])
     keep(left, lv, s_in.at[2])
     keep(mom, momv, s_in.at[3])
 
-    barrier = pltpu.get_barrier_semaphore()
-
-    def greet(m):
-        pl.semaphore_signal(barrier, inc=1, device_id=(dp, m), device_id_type=MESH)
-
-    for dy, dc in COLUMN:
-        pl.semaphore_signal(barrier, inc=1, device_id=(col(dy, dc), mp), device_id_type=MESH)
-    each_in_plane(greet)
     pl.semaphore_wait(barrier, 22)
 
-    for q in range(CHUNKS):
+    def swap(q):
         for k in range(4):
             put(
                 g.at[:, targets[k], 1 - c, pl.ds(q * ROWS, ROWS), :],
@@ -96,6 +109,7 @@
                 s_sib.at[q * 4 + k],
                 sib_dev,
             )
+            ends.append((sib.at[q, k], snd.at[0]))
 
     for j in range(4):
         ada[j] = jnp.zeros((8, 128), F32)
@@ -117,12 +131,15 @@
         return total
 
     def f0(q):
+        if q + 1 < CHUNKS:
+            swap(q + 1)
         arrived(q, 0)
         t = targets[0]
         for j in range(4):
             own[q, t, j] = both(q, 0, j).astype(BF)
         put(own.at[q, t, pl.ds(0, 2)], t1p.at[q], 1, s_t1.at[q * 2], up_dev)
         put(own.at[q, t, pl.ds(2, 2)], t1m.at[q], 1, s_t1.at[q * 2 + 1], down_dev)
+        ends.extend([(t1p.at[q], snd.at[1]), (t1m.at[q], snd.at[1])])
 
     def f1(q):
         arrived(q, 1)
@@ -141,6 +158,7 @@
                 value = value + t1m[q, j - 2].astype(F32)
             own[q, targets[2], j] = value.astype(BF)
         put(own.at[q, targets[2]], t2m.at[q], 2, s_t2.at[q * 2 + 1], down_dev)
+        ends.extend([(t2p.at[q], snd.at[2]), (t2m.at[q], snd.at[2])])
 
     def f2(q):
         arrived(q, 3)
@@ -165,18 +183,22 @@
         each_in_plane(spread)
         r, l = piece(mp)
         keep(sbuf.at[q, :, r, l], qb[q].at[pl.ds(mp * 4, 4)], s_fa.at[q])
+        ends.extend([(qb[q].at[pl.ds(0, 60)], snd.at[3]), (out_acc.at[:, rows, :], s_out.at[q])])
 
     def share_adagrad():
         ar[dp] = ada[...]
         for dy, dc in COLUMN:
             put(ada, ar.at[dp], 4, s_sm.at[0], (col(dy, dc), mp))
+        ends.append((ar.at[pl.ds(0, 7)], snd.at[4]))
 
     def f3(q):
+        if q == 0:
+            await_bytes(invv, s_inv.at[0])
         await_bytes(qb[q], s_fa.at[q])
 
         def pick(i, carry):
             for n in range(8):
-                p1[q, i * 8 + n] = qb[q][inv[i * 8 + n]]
+                p1[q, i * 8 + n] = qb[q][inv[0, i * 8 + n]]
             return carry
 
         lax.fori_loop(0, 16, pick, 0)
@@ -187,6 +209,7 @@
 
         each_in_plane(deal)
         keep(p1.at[q, pl.ds(mp * 8, 8)], vb.at[q, :, r, l], s_fb.at[q])
+        ends.append((p1.at[q, pl.ds(0, 120)], snd.at[5]))
 
     def f4(q):
         await_bytes(vb.at[q], s_fb.at[q])
@@ -194,6 +217,7 @@
             s = col(dy, dc)
             put(vb.at[q, s], gb.at[q, dp], 6, s_fc.at[q], (s, mp))
         keep(vb.at[q, dp], gb.at[q, dp], s_fc.at[q])
+        ends.append((vb.at[q, pl.ds(0, 7)], snd.at[6]))
 
     def f5(q):
         if q == 0:
@@ -209,7 +233,7 @@
 
         lax.fori_loop(0, 4, tile, 0)
 
-    def r0(q):
+    def product(q):
         if q == 0:
             await_bytes(lv, s_in.at[2])
             nrm[...] = jnp.zeros((8, 128), F32)
@@ -225,10 +249,13 @@
             return carry
 
         lax.fori_loop(0, 4, tile, 0)
+
+    def r0(q):
         for dy, dc in COLUMN:
             d = col(dy, dc)
             put(pp.at[q, d], v2.at[q, dp], 7, s_ra.at[q], (d, mp))
         keep(pp.at[q, dp], v2.at[q, dp], s_ra.at[q])
+        ends.append((pp.at[q, pl.ds(0, 7)], snd.at[7]))
 
     def share_norm():
         total = jnp.full((8, 128), jnp.sum(nrm[...]), F32)
@@ -236,6 +263,7 @@
         nv[dp] = total
         for dy, dc in COLUMN:
             put(nrm, nv.at[dp], 8, s_sm.at[1], (col(dy, dc), mp))
+        ends.append((nv.at[pl.ds(0, 7)], snd.at[8]))
 
     def spread_norms():
         await_bytes(nv.at[pl.ds(0, 7)], s_sm.at[1])
@@ -250,6 +278,7 @@
             put(nt, nw.at[mp], 9, s_sm.at[2], (dp, m))
 
         each_in_plane(send)
+        ends.append((nw.at[pl.ds(0, 15)], snd.at[9]))
 
     def r1(q):
         await_bytes(v2.at[q], s_ra.at[q])
@@ -261,13 +290,14 @@
         each_in_plane(spread)
         r, l = piece(mp)
         keep(v2.at[q, :, r, l], wb[q].at[pl.ds(mp * 8, 8)], s_rb.at[q])
+        ends.append((wb[q].at[pl.ds(0, 120)], snd.at[10]))
 
     def r2(q):
         await_bytes(wb[q], s_rb.at[q])
 
         def pick(i, carry):
             for n in range(8):
-                wp[q, i * 8 + n] = wb[q][loc[i * 8 + n]]
+                wp[q, i * 8 + n] = wb[q][place(i * 8 + n)]
             return carry
 
         lax.fori_loop(0, 8, pick, 0)
@@ -278,6 +308,7 @@
 
         each_in_plane(deal)
         keep(wp.at[q, pl.ds(mp * 4, 4)], hh.at[q, :, r, l], s_rc.at[q])
+        ends.append((wp.at[q, pl.ds(0, 60)], snd.at[11]))
 
     def scales():
         await_bytes(ar.at[pl.ds(0, 7)], s_sm.at[0])
@@ -285,9 +316,8 @@
         await_bytes(momv, s_in.at[3])
         row = lax.broadcasted_iota(jnp.int32, (8, 128), 0)
         for j in range(4):
-            place = loc[mp * 4 + j]
-            mine = nw[place // 8]
-            pre = jnp.sum(jnp.where(row == place % 8, mine, 0.0), axis=0, keepdims=True)
+            mine = nw[owner[mp * 4 + j]]
+            pre = jnp.sum(jnp.where(row == slot[mp * 4 + j], mine, 0.0), axis=0, keepdims=True)
             ada_total = jnp.sum(ar[:, j])
             scl[j] = jnp.broadcast_to(jnp.sqrt(ada_total / (pre + eps_norm)), (8, 128))
 
@@ -312,6 +342,10 @@
         put(up.at[q], rows_of(0, q), 12, s_a1.at[q * 2 + 1], down_dev)
         put(up.at[q], rows_of(0, q), 14, s_sb.at[q * 4], sib_dev)
         keep(up.at[q], rows_of(0, q), s_out.at[4 + q])
+        for k in (1, 3):
+            ends.append((rows_of(k, q), snd.at[12]))
+        ends.extend([(rows_of(0, q), snd.at[14]), (rows_of(0, q), s_out.at[4 + q])])
+        ends.append((rows_of(0, q), s_sb.at[q * 4]))
 
     def r4(q):
         await_bytes(rows_of(3, q), s_a1.at[q * 2])
@@ -320,12 +354,18 @@
         await_bytes(rows_of(1, q), s_a1.at[q * 2 + 1])
         put(rows_of(1, q, 2), rows_of(1, q, 2), 13, s_a2.at[q * 2 + 1], down_dev)
         put(rows_of(1, q), rows_of(1, q), 14, s_sb.at[q * 4 + 2], sib_dev)
+        ends.append((rows_of(2, q), snd.at[13]))
+        for k in (1, 3):
+            ends.append((rows_of(k, q), snd.at[14]))
+        ends.extend([(rows_of(3, q), s_sb.at[q * 4 + 1]), (rows_of(1, q), s_sb.at[q * 4 + 2])])
 
     def r5(q):
         await_bytes(rows_of(2, q, 0), s_a2.at[q * 2])
         await_bytes(rows_of(2, q, 2), s_a2.at[q * 2 + 1])
         put(rows_of(2, q), rows_of(2, q), 14, s_sb.at[q * 4 + 3], sib_dev)
-
+        ends.extend([(rows_of(2, q), snd.at[14]), (rows_of(2, q), s_sb.at[q * 4 + 3])])
+
+    swap(0)
     forward = (f0, f1, f2, f3, f4, f5)
     for t in range(CHUNKS + len(forward) - 1):
         for n, stage in enumerate(forward):
@@ -333,53 +373,39 @@
                 stage(t - n)
         if t == CHUNKS + 1:
             share_adagrad()
-    for q in range(CHUNKS):
-        r0(q)
+    product(0)
+    r0(0)
+    for q in range(1, CHUNKS):
+        product(q)
     share_norm()
-    back = (r1, r2, r3, r4, r5)
-    for t in range(CHUNKS + len(back) - 1):
-        if t == 1:
+    back = (r0, r1, r2, r3, r4, r5)
+    for t in range(1, CHUNKS + len(back) - 1):
+        if t == 2:
             spread_norms()
-        if t == 2:
+        if t == 3:
             scales()
         for n, stage in enumerate(back):
             if 0 <= t - n < CHUNKS:
                 stage(t - n)
 
-    for q in range(CHUNKS):
-        for k in range(4):
-            await_bytes(rows_of((0, 3, 1, 2)[k], q), s_sb.at[q * 4 + k])
-        rows = pl.ds(q * ROWS, ROWS)
-        await_bytes(out_acc.at[:, rows, :], s_out.at[q])
-        await_bytes(rows_of(0, q), s_out.at[4 + q])
-        for k in range(4):
-            await_bytes(sib.at[q, k], snd.at[0])
-            await_bytes(rows_of(k, q), snd.at[14])
-        await_bytes(t1p.at[q], snd.at[1])
-        await_bytes(t1m.at[q], snd.at[1])
-        await_bytes(t2p.at[q], snd.at[2])
-        await_bytes(t2m.at[q], snd.at[2])
-        await_bytes(qb[q].at[pl.ds(0, 60)], snd.at[3])
-        await_bytes(p1.at[q, pl.ds(0, 120)], snd.at[5])
-        await_bytes(vb.at[q, pl.ds(0, 7)], snd.at[6])
-        await_bytes(pp.at[q, pl.ds(0, 7)], snd.at[7])
-        await_bytes(wb[q].at[pl.ds(0, 120)], snd.at[10])
-        await_bytes(wp.at[q, pl.ds(0, 60)], snd.at[11])
-        await_bytes(rows_of(1, q), snd.at[12])
-        await_bytes(rows_of(3, q), snd.at[12])
-        await_bytes(rows_of(2, q), snd.at[13])
-    await_bytes(ar.at[pl.ds(0, 7)], snd.at[4])
-    await_bytes(nv.at[pl.ds(0, 7)], snd.at[8])
-    await_bytes(nw.at[pl.ds(0, 15)], snd.at[9])
+    for ref, sem in ends:
+        await_bytes(ref, sem)
+
+
+def store(acc, upd, out_acc, out_upd, sems):
+    copies = []
+    for j in range(4):
+        copies.append(pltpu.make_async_copy(acc.at[j], out_acc.at[j], sems.at[j]))
+        copies.append(pltpu.make_async_copy(upd.at[j], out_upd.at[j], sems.at[4 + j]))
+    for copy in copies:
+        copy.start()
+    for copy in copies:
+        copy.wait()
 
 
 def shards(local_grads, left_root, right_root, accumulator, momentum, block_owner, block_slot):
-    place = block_owner * 8 + block_slot
-    hit = place[None, :] == jnp.arange(128, dtype=jnp.int32)[:, None]
-    inverse = jnp.sum(
-        jnp.where(hit, jnp.arange(64, dtype=jnp.int32)[None, :], 0), axis=1, dtype=jnp.int32
-    )
     hbm = pl.BlockSpec(memory_space=pl.ANY)
+    vmem = pl.BlockSpec(memory_space=pltpu.VMEM)
     smem = pl.BlockSpec(memory_space=pltpu.SMEM)
     V = pltpu.VMEM
     dma = pltpu.SemaphoreType.DMA
@@ -400,32 +426,42 @@
         V((C, 8, R, W), BF),
         [V((128, 16, 128), BF)] * C, V((C, 64, 16, 128), BF),
         V((C, 4, R, W), BF), V((4, 8, 128), F32), V((C, 4, R, W), BF),
+        V((8, 128), jnp.int32), pltpu.SMEM((8, 128), jnp.int32),
         dma((16,)), dma((4,)), dma((16,)), dma((8,)), dma((8,)),
         dma((4,)), dma((4,)), dma((4,)), dma((4,)), dma((4,)), dma((4,)),
-        dma((3,)), dma((8,)), dma((8,)), dma((16,)), dma((8,)), dma((15,)),
+        dma((3,)), dma((8,)), dma((8,)), dma((16,)), dma((8,)), dma((1,)), dma((15,)),
     ]
     accum_new, update = pl.pallas_call(
         kernel,
-        out_shape=(
-            jax.ShapeDtypeStruct((4, 128, W), F32),
-            jax.ShapeDtypeStruct((4, 8, 128, W), BF),
-        ),
+        out_shape=(V((4, 128, W), F32), V((4, 8, 128, W), BF)),
         in_specs=[smem, smem] + [hbm] * 5,
-        out_specs=(hbm, hbm),
+        out_specs=(vmem, vmem),
         scratch_shapes=scratch,
         name="shampoo_step",
         compiler_params=pltpu.CompilerParams(
-            collective_id=0, has_side_effects=True, vmem_limit_bytes=56 * 2**20
+            collective_id=0, has_side_effects=True, vmem_limit_bytes=50 * 2**20
         ),
     )(
-        inverse,
-        place,
+        block_owner,
+        block_slot,
         local_grads.reshape(4, 4, 2, 128, W),
         left_root.reshape(8, 128, W),
         right_root.reshape(W, W),
         accumulator,
         momentum,
     )
+    accum_new, update = pl.pallas_call(
+        store,
+        out_shape=(
+            jax.ShapeDtypeStruct((4, 128, W), F32),
+            jax.ShapeDtypeStruct((4, 8, 128, W), BF),
+        ),
+        in_specs=[vmem, vmem],
+        out_specs=(hbm, hbm),
+        scratch_shapes=[dma((8,))],
+        name="store",
+        compiler_params=pltpu.CompilerParams(vmem_limit_bytes=12 * 2**20),
+    )(accum_new, update)
     return accum_new, update.reshape(4, W, W)
 
 

time: 173 us -> 150 us (0.87)
  Pallas kernels: 160 us -> 149 us
  local copies, waits for them, and re-layouts: 10.9 us -> 0 us
    unnamed x4 -> x0, local copies, waits for them, and re-layouts: 10.9 us -> none
    pallas_call x1 -> x2, Pallas kernels: 160 us -> 149 us  [the longest x1 145 us: shards(): pl.pallas_call(kernel, out_shape=(V((4, 128, W), F32), V((4, 8, 128, W),...]
where the time goes in v2:
time: 150 us
  Pallas kernels  149 us (99%)
    pallas_call x1, Pallas kernels, shards(): pl.pallas_call(kernel, out_shape=(V((4, 128, W), F32), V((4, 8, 128, W),...  145 us
    pallas_call x1, Pallas kernels, shards(): pl.pallas_call(store, out_shape=(jax.ShapeDtypeStruct((4, 128, W), F32),...  4.06 us

profile of v2, /device:TPU:1, one launch (start us, length us, event | category | flops | bytes accessed | tf_op | source)
XLA Modules:
  0.0 150.1 jit_solution(6489281547791660333)
XLA Ops:
  0.6 145.4 %shampoo_step.1 = (f32[4,128,1024]{2,1,0:T(8,128)S(1)}, bf16[4,8,128,1024]{3,2,1,0:T(8,128)(2,1)S(1)}) custom-call(s32[64]{0:T(128)} %owner.1, s32[64]{0:T(128)} %slot.1, bf16[4,4,2,128,1024]{4,3,2,1,0:T(8,128)(2,1)} %bitcast.4, bf16[8,128,1024]{2,1,0:T(8,128)(2,1)} %bitcast.5, bf16[1024,1024]{1,0:T(8,128)(2,1)} %bitcast.6, f32[4,128,1024]{2,1,0:T(8,128)} %acc.1, ...), custom_call_target="tpu_custom_call" | custom-call | tf_op jit(solution)/shard_map/shampoo_step/pallas_call | solution.py:434
  146.1 4.1 %store.1 = (f32[4,128,1024]{2,1,0:T(8,128)}, bf16[4,8,128,1024]{3,2,1,0:T(8,128)(2,1)}) custom-call(f32[4,128,1024]{2,1,0:T(8,128)S(1)} %get-tuple-element.6.acc, bf16[4,8,128,1024]{3,2,1,0:T(8,128)(2,1)S(1)} %get-tuple-element.7.upd), custom_call_target="tpu_custom_call" | custom-call | tf_op jit(solution)/shard_map/store/pallas_call | solution.py:453

commit v3 on v2

--- a/solution.py
+++ b/solution.py
@@ -14,7 +14,8 @@
 CHUNKS = 4
 ROWS = 32
 W = 1024
-COLUMN = ((2, 0), (2, 1), (1, 0), (3, 0), (1, 1), (3, 1), (0, 1))
+COLUMN = ((0, 0), (0, 1), (1, 1), (3, 1), (1, 0), (3, 0), (2, 0), (2, 1))
+NEAR, FAR = 0, 1
 PLANE = (
     (2, 2), (1, 2), (2, 1), (3, 2), (2, 3), (0, 2), (2, 0), (1, 1),
     (3, 3), (1, 3), (3, 1), (0, 1), (1, 0), (0, 3), (3, 0),
@@ -26,7 +27,7 @@
     own, sib, t1p, t1m, t2p, t2m, accv, momv, lv, rv, ada, ar, sbuf, qb, p1, vb, gb, half, pp,
     nrm, nv, nt, nw, v2, wb, wp, hh, scl, up, invv, inv,
     s_own, s_in, s_sib, s_t1, s_t2, s_fa, s_fb, s_fc, s_ra, s_rb, s_rc, s_sm,
-    s_a1, s_a2, s_sb, s_out, s_inv, snd,
+    s_a1, s_a2, s_sb, s_out, snd,
 ):
     dp = lax.axis_index("dp")
     mp = lax.axis_index("mp")
@@ -52,6 +53,13 @@
     def await_bytes(ref, sem):
         pltpu.make_async_copy(ref, ref, sem).wait()
 
+    seen_loads = set()
+
+    def loaded(ref, n):
+        if n not in seen_loads:
+            seen_loads.add(n)
+            await_bytes(ref, s_in.at[n])
+
     ends = []
 
     def place(b):
@@ -76,7 +84,7 @@
     def greet(m):
         pl.semaphore_signal(barrier, inc=1, device_id=(dp, m), device_id_type=MESH)
 
-    for dy, dc in COLUMN:
+    for dy, dc in COLUMN[1:]:
         pl.semaphore_signal(barrier, inc=1, device_id=(col(dy, dc), mp), device_id_type=MESH)
     each_in_plane(greet)
     for q in range(CHUNKS):
@@ -87,12 +95,18 @@
                 s_own.at[q * 4 + k],
             )
     lane = lax.broadcasted_iota(jnp.int32, (8, 128), 1)
+    line = lax.broadcasted_iota(jnp.int32, (8, 128), 0)
 
     def fill(b, table):
-        return jnp.where(lane == place(b), b, table)
+        dy = (y + 4 - slot[b] // 2) % 4
+        dc = (c + slot[b]) % 2
+        across = jnp.where(dc == 1, 2 + dy // 2, 4 + dy // 2)
+        seen = jnp.where(dy == 0, dc, jnp.where(dy == 2, 6 + dc, across))
+        table = jnp.where((line == 0) & (lane == place(b)), b, table)
+        return jnp.where((line == 1) & (lane == b), owner[b] * 8 + seen, table)
 
     invv[...] = lax.fori_loop(0, 64, fill, jnp.zeros((8, 128), jnp.int32))
-    keep(invv, inv, s_inv.at[0])
+    keep(invv, inv, s_in.at[4])
     keep(acc, accv, s_in.at[0])
     keep(right, rv, s_in.at[1])
     keep(left, lv, s_in.at[2])
@@ -111,6 +125,7 @@
             )
             ends.append((sib.at[q, k], snd.at[0]))
 
+    nrm[...] = jnp.zeros((8, 128), F32)
     for j in range(4):
         ada[j] = jnp.zeros((8, 128), F32)
 
@@ -164,8 +179,7 @@
         arrived(q, 3)
         await_bytes(t2p.at[q], s_t2.at[q * 2])
         await_bytes(t2m.at[q], s_t2.at[q * 2 + 1])
-        if q == 0:
-            await_bytes(accv, s_in.at[0])
+        loaded(accv, 0)
         rows = pl.ds(q * ROWS, ROWS)
         for j in range(4):
             total = both(q, 3, j) + t2p[q, j].astype(F32) + t2m[q, j].astype(F32)
@@ -187,41 +201,51 @@
 
     def share_adagrad():
         ar[dp] = ada[...]
-        for dy, dc in COLUMN:
+        for dy, dc in COLUMN[1:]:
             put(ada, ar.at[dp], 4, s_sm.at[0], (col(dy, dc), mp))
         ends.append((ar.at[pl.ds(0, 7)], snd.at[4]))
 
     def f3(q):
-        if q == 0:
-            await_bytes(invv, s_inv.at[0])
+        loaded(inv, 4)
         await_bytes(qb[q], s_fa.at[q])
 
-        def pick(i, carry):
+        def pick(o, carry):
             for n in range(8):
-                p1[q, i * 8 + n] = qb[q][inv[0, i * 8 + n]]
+                p1[q, o * 8 + n] = qb[q][inv[0, o * 8 + col(*COLUMN[n])]]
             return carry
 
         lax.fori_loop(0, 16, pick, 0)
         r, l = piece(mp)
-
-        def deal(o):
-            put(p1.at[q, pl.ds(o * 8, 8)], vb.at[q, :, r, l], 5, s_fb.at[q], (dp, o))
-
-        each_in_plane(deal)
-        keep(p1.at[q, pl.ds(mp * 8, 8)], vb.at[q, :, r, l], s_fb.at[q])
+        for part in (FAR, NEAR):
+            sem = s_fb.at[q * 2 + part]
+
+            def deal(o):
+                put(
+                    p1.at[q, pl.ds(o * 8 + part * 4, 4)],
+                    vb.at[q, pl.ds(part * 4, 4), r, l],
+                    5,
+                    sem,
+                    (dp, o),
+                )
+
+            each_in_plane(deal)
+            keep(
+                p1.at[q, pl.ds(mp * 8 + part * 4, 4)], vb.at[q, pl.ds(part * 4, 4), r, l], sem
+            )
         ends.append((p1.at[q, pl.ds(0, 120)], snd.at[5]))
 
-    def f4(q):
-        await_bytes(vb.at[q], s_fb.at[q])
-        for dy, dc in COLUMN:
-            s = col(dy, dc)
-            put(vb.at[q, s], gb.at[q, dp], 6, s_fc.at[q], (s, mp))
-        keep(vb.at[q, dp], gb.at[q, dp], s_fc.at[q])
-        ends.append((vb.at[q, pl.ds(0, 7)], snd.at[6]))
+    def f4(q, part):
+        await_bytes(vb.at[q, pl.ds(part * 4, 4)], s_fb.at[q * 2 + part])
+        for k in range(part * 4, part * 4 + 4):
+            if k:
+                put(vb.at[q, k], gb.at[q, dp], 6, s_fc.at[q], (col(*COLUMN[k]), mp))
+            else:
+                keep(vb.at[q, k], gb.at[q, dp], s_fc.at[q])
+        if part == FAR:
+            ends.append((vb.at[q, pl.ds(0, 7)], snd.at[6]))
 
     def f5(q):
-        if q == 0:
-            await_bytes(rv, s_in.at[1])
+        loaded(rv, 1)
         await_bytes(gb.at[q], s_fc.at[q])
 
         def tile(n, carry):
@@ -234,9 +258,7 @@
         lax.fori_loop(0, 4, tile, 0)
 
     def product(q):
-        if q == 0:
-            await_bytes(lv, s_in.at[2])
-            nrm[...] = jnp.zeros((8, 128), F32)
+        loaded(lv, 2)
 
         def tile(n, carry):
             lanes = pl.ds(pl.multiple_of(n * 256, 256), 256)
@@ -251,17 +273,20 @@
         lax.fori_loop(0, 4, tile, 0)
 
     def r0(q):
-        for dy, dc in COLUMN:
-            d = col(dy, dc)
-            put(pp.at[q, d], v2.at[q, dp], 7, s_ra.at[q], (d, mp))
-        keep(pp.at[q, dp], v2.at[q, dp], s_ra.at[q])
+        for k in range(8):
+            d = col(*COLUMN[k])
+            sem = s_ra.at[q * 2 + k // 4]
+            if k:
+                put(pp.at[q, d], v2.at[q, k], 7, sem, (d, mp))
+            else:
+                keep(pp.at[q, d], v2.at[q, k], sem)
         ends.append((pp.at[q, pl.ds(0, 7)], snd.at[7]))
 
     def share_norm():
         total = jnp.full((8, 128), jnp.sum(nrm[...]), F32)
         nrm[...] = total
         nv[dp] = total
-        for dy, dc in COLUMN:
+        for dy, dc in COLUMN[1:]:
             put(nrm, nv.at[dp], 8, s_sm.at[1], (col(dy, dc), mp))
         ends.append((nv.at[pl.ds(0, 7)], snd.at[8]))
 
@@ -280,24 +305,26 @@
         each_in_plane(send)
         ends.append((nw.at[pl.ds(0, 15)], snd.at[9]))
 
-    def r1(q):
-        await_bytes(v2.at[q], s_ra.at[q])
+    def r1(q, part):
+        slots = pl.ds(part * 4, 4)
+        await_bytes(v2.at[q, slots], s_ra.at[q * 2 + part])
+        into = pl.ds(mp * 8 + part * 4, 4)
 
         def spread(m):
             r, l = piece(m)
-            put(v2.at[q, :, r, l], wb[q].at[pl.ds(mp * 8, 8)], 10, s_rb.at[q], (dp, m))
+            put(v2.at[q, slots, r, l], wb[q].at[into], 10, s_rb.at[q], (dp, m))
 
         each_in_plane(spread)
         r, l = piece(mp)
-        keep(v2.at[q, :, r, l], wb[q].at[pl.ds(mp * 8, 8)], s_rb.at[q])
-        ends.append((wb[q].at[pl.ds(0, 120)], snd.at[10]))
+        keep(v2.at[q, slots, r, l], wb[q].at[into], s_rb.at[q])
+        ends.append((wb[q].at[pl.ds(0, 60)], snd.at[10]))
 
     def r2(q):
         await_bytes(wb[q], s_rb.at[q])
 
         def pick(i, carry):
             for n in range(8):
-                wp[q, i * 8 + n] = wb[q][place(i * 8 + n)]
+                wp[q, i * 8 + n] = wb[q][inv[1, i * 8 + n]]
             return carry
 
         lax.fori_loop(0, 8, pick, 0)
@@ -313,7 +340,7 @@
     def scales():
         await_bytes(ar.at[pl.ds(0, 7)], s_sm.at[0])
         await_bytes(nw.at[pl.ds(0, 15)], s_sm.at[2])
-        await_bytes(momv, s_in.at[3])
+        loaded(momv, 3)
         row = lax.broadcasted_iota(jnp.int32, (8, 128), 0)
         for j in range(4):
             mine = nw[owner[mp * 4 + j]]
@@ -321,72 +348,62 @@
             ada_total = jnp.sum(ar[:, j])
             scl[j] = jnp.broadcast_to(jnp.sqrt(ada_total / (pre + eps_norm)), (8, 128))
 
-    def group(dy):
-        return col(dy, 0)
-
-    def rows_of(dy, q, blocks=None):
-        if blocks is None:
-            return out_upd.at[:, group(dy), pl.ds(q * ROWS, ROWS), :]
-        return out_upd.at[pl.ds(blocks, 2), group(dy), pl.ds(q * ROWS, ROWS), :]
-
-    def r3(q):
-        await_bytes(hh.at[q], s_rc.at[q])
-        for j in range(4):
+    def rows_of(dy, q, first, count):
+        return out_upd.at[pl.ds(first, count), col(dy, 0), pl.ds(q * ROWS, ROWS), :]
+
+    def r3(q, first, count):
+        if first == 0:
+            await_bytes(hh.at[q], s_rc.at[q])
+        for j in range(first, first + count):
             scale = jnp.concatenate([scl[j, 0:1, :]] * 8, axis=1)
             value = (
                 beta_momentum * momv[j, pl.ds(q * ROWS, ROWS), :].astype(F32)
                 + scale * hh[q, j].astype(F32)
             )
             up[q, j] = value.astype(BF)
-        put(up.at[q], rows_of(0, q), 12, s_a1.at[q * 2], up_dev)
-        put(up.at[q], rows_of(0, q), 12, s_a1.at[q * 2 + 1], down_dev)
-        put(up.at[q], rows_of(0, q), 14, s_sb.at[q * 4], sib_dev)
-        keep(up.at[q], rows_of(0, q), s_out.at[4 + q])
-        for k in (1, 3):
-            ends.append((rows_of(k, q), snd.at[12]))
-        ends.extend([(rows_of(0, q), snd.at[14]), (rows_of(0, q), s_out.at[4 + q])])
-        ends.append((rows_of(0, q), s_sb.at[q * 4]))
-
-    def r4(q):
-        await_bytes(rows_of(3, q), s_a1.at[q * 2])
-        put(rows_of(3, q, 0), rows_of(3, q, 0), 13, s_a2.at[q * 2], up_dev)
-        put(rows_of(3, q), rows_of(3, q), 14, s_sb.at[q * 4 + 1], sib_dev)
-        await_bytes(rows_of(1, q), s_a1.at[q * 2 + 1])
-        put(rows_of(1, q, 2), rows_of(1, q, 2), 13, s_a2.at[q * 2 + 1], down_dev)
-        put(rows_of(1, q), rows_of(1, q), 14, s_sb.at[q * 4 + 2], sib_dev)
-        ends.append((rows_of(2, q), snd.at[13]))
-        for k in (1, 3):
-            ends.append((rows_of(k, q), snd.at[14]))
-        ends.extend([(rows_of(3, q), s_sb.at[q * 4 + 1]), (rows_of(1, q), s_sb.at[q * 4 + 2])])
-
-    def r5(q):
-        await_bytes(rows_of(2, q, 0), s_a2.at[q * 2])
-        await_bytes(rows_of(2, q, 2), s_a2.at[q * 2 + 1])
-        put(rows_of(2, q), rows_of(2, q), 14, s_sb.at[q * 4 + 3], sib_dev)
-        ends.extend([(rows_of(2, q), snd.at[14]), (rows_of(2, q), s_sb.at[q * 4 + 3])])
+        n = q * 2 + first // 2
+        mine = up.at[q, pl.ds(first, count)]
+        here = rows_of(0, q, first, count)
+        put(mine, here, 12, s_a1.at[n * 2], up_dev)
+        put(mine, here, 12, s_a1.at[n * 2 + 1], down_dev)
+        put(mine, here, 14, s_sb.at[n * 4], sib_dev)
+        keep(mine, here, s_out.at[4 + n])
+        ends.extend([(here, snd.at[12]), (here, snd.at[12]), (here, snd.at[14])])
+        ends.extend([(here, s_out.at[4 + n]), (here, s_sb.at[n * 4])])
+
+    def r4(q, first, count):
+        n = q * 2 + first // 2
+        for k, dy in ((0, 3), (1, 1)):
+            rows = rows_of(dy, q, first, count)
+            await_bytes(rows, s_a1.at[n * 2 + k])
+            part = rows_of(dy, q, first + k * (count // 2), count // 2)
+            put(part, part, 13, s_a2.at[n * 2 + k], (up_dev, down_dev)[k])
+            put(rows, rows, 14, s_sb.at[n * 4 + 1 + k], sib_dev)
+            ends.extend([(part, snd.at[13]), (rows, snd.at[14]), (rows, s_sb.at[n * 4 + 1 + k])])
+
+    def r5(q, first, count):
+        n = q * 2 + first // 2
+        for k in range(2):
+            part = rows_of(2, q, first + k * (count // 2), count // 2)
+            await_bytes(part, s_a2.at[n * 2 + k])
+        rows = rows_of(2, q, first, count)
+        put(rows, rows, 14, s_sb.at[n * 4 + 3], sib_dev)
+        ends.extend([(rows, snd.at[14]), (rows, s_sb.at[n * 4 + 3])])
 
     swap(0)
-    forward = (f0, f1, f2, f3, f4, f5)
-    for t in range(CHUNKS + len(forward) - 1):
-        for n, stage in enumerate(forward):
-            if 0 <= t - n < CHUNKS:
-                stage(t - n)
-        if t == CHUNKS + 1:
-            share_adagrad()
-    product(0)
-    r0(0)
-    for q in range(1, CHUNKS):
-        product(q)
-    share_norm()
-    back = (r0, r1, r2, r3, r4, r5)
-    for t in range(1, CHUNKS + len(back) - 1):
-        if t == 2:
-            spread_norms()
-        if t == 3:
-            scales()
-        for n, stage in enumerate(back):
-            if 0 <= t - n < CHUNKS:
-                stage(t - n)
+    for stage, *which in (
+        (f0, 0), (f0, 1), (f1, 0), (f1, 1), (f0, 2), (f0, 3), (f2, 0), (f2, 1), (f1, 2), (f3, 0),
+        (f3, 1), (f1, 3), (f2, 2), (f4, 0, FAR), (f2, 3), (share_adagrad,), (f4, 0, NEAR),
+        (f4, 1, FAR), (f4, 1, NEAR), (f3, 2), (f4, 2, FAR), (f3, 3), (f5, 1), (f4, 2, NEAR),
+        (f4, 3, FAR), (f5, 0), (f4, 3, NEAR), (f5, 2), (f5, 3),
+        (product, 0), (r0, 0), (product, 1), (product, 2), (product, 3), (share_norm,), (r0, 1),
+        (r0, 2), (r1, 0, NEAR), (r0, 3), (r1, 0, FAR), (r1, 1, NEAR), (spread_norms,), (r2, 0),
+        (r1, 1, FAR), (scales,), (r3, 0, 0, 4), (r1, 2, FAR), (r2, 1), (r1, 2, NEAR),
+        (r1, 3, FAR), (r3, 1, 0, 4), (r4, 0, 0, 4), (r2, 2), (r1, 3, NEAR), (r4, 1, 0, 4),
+        (r3, 2, 0, 4), (r2, 3), (r3, 3, 0, 2), (r3, 3, 2, 2), (r4, 2, 0, 4), (r4, 3, 0, 2),
+        (r5, 0, 0, 4), (r4, 3, 2, 2), (r5, 2, 0, 4), (r5, 1, 0, 4), (r5, 3, 0, 2), (r5, 3, 2, 2),
+    ):
+        stage(*which)
 
     for ref, sem in ends:
         await_bytes(ref, sem)
@@ -427,9 +444,9 @@
         [V((128, 16, 128), BF)] * C, V((C, 64, 16, 128), BF),
         V((C, 4, R, W), BF), V((4, 8, 128), F32), V((C, 4, R, W), BF),
         V((8, 128), jnp.int32), pltpu.SMEM((8, 128), jnp.int32),
-        dma((16,)), dma((4,)), dma((16,)), dma((8,)), dma((8,)),
-        dma((4,)), dma((4,)), dma((4,)), dma((4,)), dma((4,)), dma((4,)),
-        dma((3,)), dma((8,)), dma((8,)), dma((16,)), dma((8,)), dma((1,)), dma((15,)),
+        dma((16,)), dma((5,)), dma((16,)), dma((8,)), dma((8,)),
+        dma((4,)), dma((8,)), dma((4,)), dma((8,)), dma((4,)), dma((4,)),
+        dma((3,)), dma((16,)), dma((16,)), dma((32,)), dma((12,)), dma((15,)),
     ]
     accum_new, update = pl.pallas_call(
         kernel,

time: 150 us -> 142 us (0.947)
  Pallas kernels: 149 us -> 141 us
    pallas_call x1, Pallas kernels: 145 us -> 137 us  [shards(): pl.pallas_call(kernel, out_shape=(V((4, 128, W), F32), V((4, 8, 128, W),...]
where the time goes in v3:
time: 142 us
  Pallas kernels  141 us (99%)
    pallas_call x1, Pallas kernels, shards(): pl.pallas_call(kernel, out_shape=(V((4, 128, W), F32), V((4, 8, 128, W),...  137 us
    pallas_call x1, Pallas kernels, shards(): pl.pallas_call(store, out_shape=(jax.ShapeDtypeStruct((4, 128, W), F32),...  4.06 us

profile of v3, /device:TPU:1, one launch (start us, length us, event | category | flops | bytes accessed | tf_op | source)
XLA Modules:
  0.0 142.0 jit_solution(5173850440271517648)
XLA Ops:
  0.6 137.3 %shampoo_step.1 = (f32[4,128,1024]{2,1,0:T(8,128)S(1)}, bf16[4,8,128,1024]{3,2,1,0:T(8,128)(2,1)S(1)}) custom-call(s32[64]{0:T(128)} %owner.1, s32[64]{0:T(128)} %slot.1, bf16[4,4,2,128,1024]{4,3,2,1,0:T(8,128)(2,1)} %bitcast.4, bf16[8,128,1024]{2,1,0:T(8,128)(2,1)} %bitcast.5, bf16[1024,1024]{1,0:T(8,128)(2,1)} %bitcast.6, f32[4,128,1024]{2,1,0:T(8,128)} %acc.1, ...), custom_call_target="tpu_custom_call" | custom-call | tf_op jit(solution)/shard_map/shampoo_step/pallas_call | solution.py:451
  138.0 4.1 %store.1 = (f32[4,128,1024]{2,1,0:T(8,128)}, bf16[4,8,128,1024]{3,2,1,0:T(8,128)(2,1)}) custom-call(f32[4,128,1024]{2,1,0:T(8,128)S(1)} %get-tuple-element.6.acc, bf16[4,8,128,1024]{3,2,1,0:T(8,128)(2,1)S(1)} %get-tuple-element.7.upd), custom_call_target="tpu_custom_call" | custom-call | tf_op jit(solution)/shard_map/store/pallas_call | solution.py:470

commit v4 on v3

--- a/solution.py
+++ b/solution.py
@@ -12,6 +12,7 @@
 eps_norm = 1e-06
 
 CHUNKS = 4
+TILE = 512
 ROWS = 32
 W = 1024
 COLUMN = ((0, 0), (0, 1), (1, 1), (3, 1), (1, 0), (3, 0), (2, 0), (2, 1))
@@ -24,7 +25,7 @@
 
 def kernel(
     owner, slot, g, left, right, acc, mom, out_acc, out_upd,
-    own, sib, t1p, t1m, t2p, t2m, accv, momv, lv, rv, ada, ar, sbuf, qb, p1, vb, gb, half, pp,
+    own, sib, t1p, t1m, t2p, t2m, accv, momv, lv, rv, ada, adt, ar, sbuf, qb, p1, vb, gb, half, pp,
     nrm, nv, nt, nw, v2, wb, wp, hh, scl, up, invv, inv,
     s_own, s_in, s_sib, s_t1, s_t2, s_fa, s_fb, s_fc, s_ra, s_rb, s_rc, s_sm,
     s_a1, s_a2, s_sb, s_out, snd,
@@ -200,9 +201,14 @@
         ends.extend([(qb[q].at[pl.ds(0, 60)], snd.at[3]), (out_acc.at[:, rows, :], s_out.at[q])])
 
     def share_adagrad():
-        ar[dp] = ada[...]
+        row = lax.broadcasted_iota(jnp.int32, (8, 128), 0)
+        table = jnp.zeros((8, 128), F32)
+        for j in range(4):
+            table = jnp.where(row == j, jnp.sum(ada[j]), table)
+        adt[...] = table
+        ar[dp] = table
         for dy, dc in COLUMN[1:]:
-            put(ada, ar.at[dp], 4, s_sm.at[0], (col(dy, dc), mp))
+            put(adt, ar.at[dp], 4, s_sm.at[0], (col(dy, dc), mp))
         ends.append((ar.at[pl.ds(0, 7)], snd.at[4]))
 
     def f3(q):
@@ -244,66 +250,85 @@
         if part == FAR:
             ends.append((vb.at[q, pl.ds(0, 7)], snd.at[6]))
 
+    def half_tile(q, lanes):
+        rows = gb[q].reshape(8 * ROWS, W)
+        value = jnp.dot(rows, rv[:, lanes], preferred_element_type=F32)
+        half[:, pl.ds(q * ROWS, ROWS), lanes] = value.astype(BF).reshape(8, ROWS, TILE)
+
+    def product_tile(q, lanes):
+        rows = lv[:, pl.ds(q * ROWS, ROWS), :].reshape(8 * ROWS, W)
+        value = jnp.dot(rows, half[:, :, lanes].reshape(W, TILE), preferred_element_type=F32)
+        value = value.astype(BF)
+        pp[q, :, :, lanes] = value.reshape(8, ROWS, TILE)
+        wide = value.astype(F32)
+        nrm[...] += fold(wide * wide)
+
+    def by_tiles(body, q):
+        def step(n, carry):
+            body(q, pl.ds(pl.multiple_of(n * TILE, TILE), TILE))
+            return carry
+
+        lax.fori_loop(0, W // TILE, step, 0)
+
     def f5(q):
         loaded(rv, 1)
         await_bytes(gb.at[q], s_fc.at[q])
-
-        def tile(n, carry):
-            lanes = pl.ds(pl.multiple_of(n * 256, 256), 256)
-            rows = gb[q].reshape(8 * ROWS, W)
-            value = jnp.dot(rows, rv[:, lanes], preferred_element_type=F32)
-            half[:, pl.ds(q * ROWS, ROWS), lanes] = value.astype(BF).reshape(8, ROWS, 256)
-            return carry
-
-        lax.fori_loop(0, 4, tile, 0)
+        by_tiles(half_tile, q)
 
     def product(q):
-        loaded(lv, 2)
-
-        def tile(n, carry):
-            lanes = pl.ds(pl.multiple_of(n * 256, 256), 256)
-            rows = lv[:, pl.ds(q * ROWS, ROWS), :].reshape(8 * ROWS, W)
-            value = jnp.dot(rows, half[:, :, lanes].reshape(W, 256), preferred_element_type=F32)
-            value = value.astype(BF)
-            pp[q, :, :, lanes] = value.reshape(8, ROWS, 256)
-            wide = value.astype(F32)
-            nrm[...] += fold(wide * wide)
-            return carry
-
-        lax.fori_loop(0, 4, tile, 0)
-
-    def r0(q):
-        for k in range(8):
+        by_tiles(product_tile, q)
+
+    def give(q, ks, lanes):
+        for k in ks:
             d = col(*COLUMN[k])
             sem = s_ra.at[q * 2 + k // 4]
             if k:
-                put(pp.at[q, d], v2.at[q, k], 7, sem, (d, mp))
+                put(pp.at[q, d, :, lanes], v2.at[q, k, :, lanes], 7, sem, (d, mp))
             else:
-                keep(pp.at[q, d], v2.at[q, k], sem)
+                keep(pp.at[q, d, :, lanes], v2.at[q, k, :, lanes], sem)
+
+    def r0(q):
+        give(q, range(8), pl.ds(0, W))
         ends.append((pp.at[q, pl.ds(0, 7)], snd.at[7]))
 
+    def turn(q):
+        loaded(lv, 2)
+        await_bytes(gb.at[q], s_fc.at[q])
+        first, second = pl.ds(0, TILE), pl.ds(TILE, TILE)
+        half_tile(q, first)
+        product_tile(0, first)
+        give(0, range(6), first)
+        half_tile(q, second)
+        product_tile(0, second)
+        give(0, range(4), second)
+        give(0, (6, 7), first)
+        give(0, range(4, 8), second)
+        ends.append((pp.at[0, pl.ds(0, 7)], snd.at[7]))
+
+    line0 = pl.ds(0, 1)
+
     def share_norm():
-        total = jnp.full((8, 128), jnp.sum(nrm[...]), F32)
-        nrm[...] = total
-        nv[dp] = total
+        total = jnp.full((1, 128), jnp.sum(nrm[...]), F32)
+        nrm[0:1, :] = total
+        nv[dp, 0:1, :] = total
         for dy, dc in COLUMN[1:]:
-            put(nrm, nv.at[dp], 8, s_sm.at[1], (col(dy, dc), mp))
-        ends.append((nv.at[pl.ds(0, 7)], snd.at[8]))
+            put(nrm.at[line0], nv.at[dp, line0], 8, s_sm.at[1], (col(dy, dc), mp))
+        ends.append((nv.at[pl.ds(0, 7), line0], snd.at[8]))
 
     def spread_norms():
-        await_bytes(nv.at[pl.ds(0, 7)], s_sm.at[1])
-        row = lax.broadcasted_iota(jnp.int32, (8, 128), 0)
-        table = jnp.zeros((8, 128), F32)
+        await_bytes(nv.at[pl.ds(0, 7), line0], s_sm.at[1])
+        at = lax.broadcasted_iota(jnp.int32, (1, 128), 1)
+        table = jnp.zeros((1, 128), F32)
         for s in range(8):
-            table = jnp.where(row == s, nv[s], table)
-        nt[...] = table
-        nw[mp] = table
+            table = jnp.where(at == s, nv[s, 0:1, :], table)
+        nt[0:1, :] = table
+        nw[mp, 0:1, :] = table
 
         def send(m):
-            put(nt, nw.at[mp], 9, s_sm.at[2], (dp, m))
+            put(nt.at[line0], nw.at[mp, line0], 9, s_sm.at[2], (dp, m))
 
         each_in_plane(send)
-        ends.append((nw.at[pl.ds(0, 15)], snd.at[9]))
+        ends.append((nw.at[pl.ds(0, 15), line0], snd.at[9]))
 
     def r1(q, part):
         slots = pl.ds(part * 4, 4)
@@ -339,14 +364,15 @@
 
     def scales():
         await_bytes(ar.at[pl.ds(0, 7)], s_sm.at[0])
-        await_bytes(nw.at[pl.ds(0, 15)], s_sm.at[2])
+        await_bytes(nw.at[pl.ds(0, 15), line0], s_sm.at[2])
         loaded(momv, 3)
-        row = lax.broadcasted_iota(jnp.int32, (8, 128), 0)
+        at = lax.broadcasted_iota(jnp.int32, (1, 128), 1)
+        sums = jnp.sum(ar[...], axis=0)
         for j in range(4):
-            mine = nw[owner[mp * 4 + j]]
-            pre = jnp.sum(jnp.where(row == slot[mp * 4 + j], mine, 0.0), axis=0, keepdims=True)
-            ada_total = jnp.sum(ar[:, j])
-            scl[j] = jnp.broadcast_to(jnp.sqrt(ada_total / (pre + eps_norm)), (8, 128))
+            mine = nw[owner[mp * 4 + j], 0:1, :]
+            pre = jnp.sum(jnp.where(at == slot[mp * 4 + j], mine, 0.0), axis=1, keepdims=True)
+            scale = jnp.sqrt(sums[j : j + 1, :] / (pre + eps_norm))
+            scl[j] = jnp.broadcast_to(scale, (8, 128))
 
     def rows_of(dy, q, first, count):
         return out_upd.at[pl.ds(first, count), col(dy, 0), pl.ds(q * ROWS, ROWS), :]
@@ -393,10 +419,11 @@
     swap(0)
     for stage, *which in (
         (f0, 0), (f0, 1), (f1, 0), (f1, 1), (f0, 2), (f0, 3), (f2, 0), (f2, 1), (f1, 2), (f3, 0),
-        (f3, 1), (f1, 3), (f2, 2), (f4, 0, FAR), (f2, 3), (share_adagrad,), (f4, 0, NEAR),
+        (f3, 1), (f1, 3), (f2, 2), (f4, 0, FAR), (f2, 3), (f4, 0, NEAR),
         (f4, 1, FAR), (f4, 1, NEAR), (f3, 2), (f4, 2, FAR), (f3, 3), (f5, 1), (f4, 2, NEAR),
-        (f4, 3, FAR), (f5, 0), (f4, 3, NEAR), (f5, 2), (f5, 3),
-        (product, 0), (r0, 0), (product, 1), (product, 2), (product, 3), (share_norm,), (r0, 1),
+        (f4, 3, FAR), (f5, 0), (f4, 3, NEAR), (share_adagrad,), (f5, 2),
+        (turn, 3),
+        (product, 1), (product, 2), (product, 3), (share_norm,), (r0, 1),
         (r0, 2), (r1, 0, NEAR), (r0, 3), (r1, 0, FAR), (r1, 1, NEAR), (spread_norms,), (r2, 0),
         (r1, 1, FAR), (scales,), (r3, 0, 0, 4), (r1, 2, FAR), (r2, 1), (r1, 2, NEAR),
         (r1, 3, FAR), (r3, 1, 0, 4), (r4, 0, 0, 4), (r2, 2), (r1, 3, NEAR), (r4, 1, 0, 4),
@@ -433,7 +460,7 @@
         V((C, 4, R, W), BF), V((C, 4, R, W), BF),
         V((4, 128, W), F32), V((4, 128, W), BF),
         V((8, 128, W), BF), V((W, W), BF),
-        V((4, 8, 128), F32), V((8, 4, 8, 128), F32),
+        V((4, 8, 128), F32), V((8, 128), F32), V((8, 8, 128), F32),
         V((C, 4, R, W), BF),
         [V((64, 16, 128), BF)] * C, V((C, 128, 16, 128), BF),
         V((C, 8, R, W), BF), V((C, 8, R, W), BF),

time: 142 us -> 140 us (0.986)
  Pallas kernels: 141 us -> 139 us
    pallas_call x1, Pallas kernels: 137 us -> 135 us  [shards(): pl.pallas_call(kernel, out_shape=(V((4, 128, W), F32), V((4, 8, 128, W),...]
where the time goes in v4:
time: 140 us
  Pallas kernels  139 us (99%)
    pallas_call x1, Pallas kernels, shards(): pl.pallas_call(kernel, out_shape=(V((4, 128, W), F32), V((4, 8, 128, W),...  135 us
    pallas_call x1, Pallas kernels, shards(): pl.pallas_call(store, out_shape=(jax.ShapeDtypeStruct((4, 128, W), F32),...  4.06 us

profile of v4, /device:TPU:1, one launch (start us, length us, event | category | flops | bytes accessed | tf_op | source)
XLA Modules:
  0.0 139.9 jit_solution(10466578005772383676)
XLA Ops:
  0.6 135.2 %shampoo_step.1 = (f32[4,128,1024]{2,1,0:T(8,128)S(1)}, bf16[4,8,128,1024]{3,2,1,0:T(8,128)(2,1)S(1)}) custom-call(s32[64]{0:T(128)} %owner.1, s32[64]{0:T(128)} %slot.1, bf16[4,4,2,128,1024]{4,3,2,1,0:T(8,128)(2,1)} %bitcast.4, bf16[8,128,1024]{2,1,0:T(8,128)(2,1)} %bitcast.5, bf16[1024,1024]{1,0:T(8,128)(2,1)} %bitcast.6, f32[4,128,1024]{2,1,0:T(8,128)} %acc.1, ...), custom_call_target="tpu_custom_call" | custom-call | tf_op jit(solution)/shard_map/shampoo_step/pallas_call | solution.py:478
  135.8 4.1 %store.1 = (f32[4,128,1024]{2,1,0:T(8,128)}, bf16[4,8,128,1024]{3,2,1,0:T(8,128)(2,1)}) custom-call(f32[4,128,1024]{2,1,0:T(8,128)S(1)} %get-tuple-element.6.acc, bf16[4,8,128,1024]{3,2,1,0:T(8,128)(2,1)S(1)} %get-tuple-element.7.upd), custom_call_target="tpu_custom_call" | custom-call | tf_op jit(solution)/shard_map/store/pallas_call | solution.py:497

commit v5 on v4

--- a/solution.py
+++ b/solution.py
@@ -40,7 +40,7 @@
         return ((y + dy) % 4) * 2 + (c + dc) % 2
 
     def plane(dz, dx):
-        return ((z + dz) % 4) * 4 + (x + dx) % 4
+        return ((z + dz + c * (4 + dx - dz)) % 4) * 4 + (x + dx + c * (4 + dz - dx)) % 4
 
     def put(src, dst, ssem, rsem, device):
         pltpu.make_async_remote_copy(

time: 140 us -> 138 us (0.986)
  Pallas kernels: 139 us -> 137 us
    pallas_call x1, Pallas kernels: 135 us -> 133 us  [shards(): pl.pallas_call(kernel, out_shape=(V((4, 128, W), F32), V((4, 8, 128, W),...]
where the time goes in v5:
time: 138 us
  Pallas kernels  137 us (99%)
    pallas_call x1, Pallas kernels, shards(): pl.pallas_call(kernel, out_shape=(V((4, 128, W), F32), V((4, 8, 128, W),...  133 us
    pallas_call x1, Pallas kernels, shards(): pl.pallas_call(store, out_shape=(jax.ShapeDtypeStruct((4, 128, W), F32),...  4.06 us

profile of v5, /device:TPU:1, one launch (start us, length us, event | category | flops | bytes accessed | tf_op | source)
XLA Modules:
  0.0 137.7 jit_solution(13412922310445622561)
XLA Ops:
  0.6 133.0 %shampoo_step.1 = (f32[4,128,1024]{2,1,0:T(8,128)S(1)}, bf16[4,8,128,1024]{3,2,1,0:T(8,128)(2,1)S(1)}) custom-call(s32[64]{0:T(128)} %owner.1, s32[64]{0:T(128)} %slot.1, bf16[4,4,2,128,1024]{4,3,2,1,0:T(8,128)(2,1)} %bitcast.4, bf16[8,128,1024]{2,1,0:T(8,128)(2,1)} %bitcast.5, bf16[1024,1024]{1,0:T(8,128)(2,1)} %bitcast.6, f32[4,128,1024]{2,1,0:T(8,128)} %acc.1, ...), custom_call_target="tpu_custom_call" | custom-call | tf_op jit(solution)/shard_map/shampoo_step/pallas_call | solution.py:478
  133.7 4.1 %store.1 = (f32[4,128,1024]{2,1,0:T(8,128)}, bf16[4,8,128,1024]{3,2,1,0:T(8,128)(2,1)}) custom-call(f32[4,128,1024]{2,1,0:T(8,128)S(1)} %get-tuple-element.6.acc, bf16[4,8,128,1024]{3,2,1,0:T(8,128)(2,1)S(1)} %get-tuple-element.7.upd), custom_call_target="tpu_custom_call" | custom-call | tf_op jit(solution)/shard_map/store/pallas_call | solution.py:497

commit v6 on v5

--- a/solution.py
+++ b/solution.py
@@ -416,6 +416,12 @@
         put(rows, rows, 14, s_sb.at[n * 4 + 3], sib_dev)
         ends.extend([(rows, snd.at[14]), (rows, s_sb.at[n * 4 + 3])])
 
+    def settle(keep_last=0):
+        early = ends[: len(ends) - keep_last]
+        del ends[: len(early)]
+        for ref, sem in early:
+            await_bytes(ref, sem)
+
     swap(0)
     for stage, *which in (
         (f0, 0), (f0, 1), (f1, 0), (f1, 1), (f0, 2), (f0, 3), (f2, 0), (f2, 1), (f1, 2), (f3, 0),
@@ -424,10 +430,10 @@
         (f4, 3, FAR), (f5, 0), (f4, 3, NEAR), (share_adagrad,), (f5, 2),
         (turn, 3),
         (product, 1), (product, 2), (product, 3), (share_norm,), (r0, 1),
-        (r0, 2), (r1, 0, NEAR), (r0, 3), (r1, 0, FAR), (r1, 1, NEAR), (spread_norms,), (r2, 0),
+        (r0, 2), (r1, 0, NEAR), (r0, 3), (settle, 6), (r1, 0, FAR), (r1, 1, NEAR), (spread_norms,), (r2, 0),
         (r1, 1, FAR), (scales,), (r3, 0, 0, 4), (r1, 2, FAR), (r2, 1), (r1, 2, NEAR),
         (r1, 3, FAR), (r3, 1, 0, 4), (r4, 0, 0, 4), (r2, 2), (r1, 3, NEAR), (r4, 1, 0, 4),
-        (r3, 2, 0, 4), (r2, 3), (r3, 3, 0, 2), (r3, 3, 2, 2), (r4, 2, 0, 4), (r4, 3, 0, 2),
+        (r3, 2, 0, 4), (r2, 3), (r3, 3, 0, 2), (r3, 3, 2, 2), (settle, 45), (r4, 2, 0, 4), (r4, 3, 0, 2),
         (r5, 0, 0, 4), (r4, 3, 2, 2), (r5, 2, 0, 4), (r5, 1, 0, 4), (r5, 3, 0, 2), (r5, 3, 2, 2),
     ):
         stage(*which)

time: 138 us -> 138 us (level)
  no operation moved by 1% of the time
where the time goes in v6:
time: 138 us
  Pallas kernels  137 us (99%)
    pallas_call x1, Pallas kernels, shards(): pl.pallas_call(kernel, out_shape=(V((4, 128, W), F32), V((4, 8, 128, W),...  133 us
    pallas_call x1, Pallas kernels, shards(): pl.pallas_call(store, out_shape=(jax.ShapeDtypeStruct((4, 128, W), F32),...  4.06 us

profile of v6, /device:TPU:1, one launch (start us, length us, event | category | flops | bytes accessed | tf_op | source)
XLA Modules:
  0.0 137.7 jit_solution(16794759615631184843)
XLA Ops:
  0.6 133.0 %shampoo_step.1 = (f32[4,128,1024]{2,1,0:T(8,128)S(1)}, bf16[4,8,128,1024]{3,2,1,0:T(8,128)(2,1)S(1)}) custom-call(s32[64]{0:T(128)} %owner.1, s32[64]{0:T(128)} %slot.1, bf16[4,4,2,128,1024]{4,3,2,1,0:T(8,128)(2,1)} %bitcast.4, bf16[8,128,1024]{2,1,0:T(8,128)(2,1)} %bitcast.5, bf16[1024,1024]{1,0:T(8,128)(2,1)} %bitcast.6, f32[4,128,1024]{2,1,0:T(8,128)} %acc.1, ...), custom_call_target="tpu_custom_call" | custom-call | tf_op jit(solution)/shard_map/shampoo_step/pallas_call | solution.py:484
  133.7 4.1 %store.1 = (f32[4,128,1024]{2,1,0:T(8,128)}, bf16[4,8,128,1024]{3,2,1,0:T(8,128)(2,1)}) custom-call(f32[4,128,1024]{2,1,0:T(8,128)S(1)} %get-tuple-element.6.acc, bf16[4,8,128,1024]{3,2,1,0:T(8,128)(2,1)S(1)} %get-tuple-element.7.upd), custom_call_target="tpu_custom_call" | custom-call | tf_op jit(solution)/shard_map/store/pallas_call | solution.py:503
